TPU v7x, 768 devices: a whole 4x8x12 slice. The times are simulated.
768 devices in a mesh: dp: 12 (over z), mp: 64 (over x, y, core).
Axes of the slice: x: 4, y: 8, z: 12, core: 2. Of those that a mesh axis runs over, the one named last changes fastest.
Arguments:
- query_states: bfloat16 [98304, 1024], P(('dp', 'mp')), may hold values from -6 to 6
- passage_states: bfloat16 [1105920, 1024], P(('dp', 'mp')), may hold values from -6 to 6
- proj_weight: bfloat16 [1024, 128], P('mp'), may hold values from -0.1875 to 0.1875
- negatives: int32 [3072, 32], P(('dp', 'mp')), may hold values from 0 to 6143, as said below
- ranks: int32 [3072, 32], P(('dp', 'mp')), may hold values from 0 to 31, each once within a row
Outputs:
- grad_queries: bfloat16 [98304, 1024], P(('dp', 'mp'))
- grad_weight: float32 [1024, 128], P('mp')
Inputs may be any that keep to these rules, and one draw needn't show every extreme that they name: `negatives`: each row lists 32 different passages. Passage g is held by the device of index g // 8 in dp+mp order, and every listed passage of a query is held by a device whose mp index equals that of the query's own device. `ranks`: each row holds every rank of 0 to 31 once.
All inputs are finite; a program needn't handle non-finite values.
Results may differ from a plain program's by a relative error of at most 0.025.
Values may be sent and summed in bfloat16 or wider, within the bound.
No kernel may reach another device: no remote copies, remote signals or barrier semaphores. Data moves between devices by JAX's collectives and lax.ppermute only.
A program may use at most 128 MiB of HBM per device.

v0:
```python
import jax
import jax.numpy as jnp
from jax import lax
from jax.sharding import PartitionSpec as P

QLEN = 32
PLEN = 180


TAU = 0.1
RANK_TEMP = 8.0
EPS = 1e-06


def normalize(values):
    scale = lax.rsqrt(jnp.sum(values * values, axis=-1, keepdims=True) + EPS)
    return (values * scale, scale)


def on_device(query_states, passage_states, proj_weight, negatives, ranks):
    weight = lax.all_gather(proj_weight, "mp", axis=0, tiled=True)
    eq, rq = normalize(jnp.dot(query_states, weight, preferred_element_type=jnp.float32))
    ep, rp = normalize(jnp.dot(passage_states, weight, preferred_element_type=jnp.float32))
    eqb = eq.astype(jnp.bfloat16)
    epflat = ep.astype(jnp.bfloat16)
    allq = lax.all_gather(eqb, "dp", axis=0, tiled=True)
    groups = lax.axis_size("dp")
    here = lax.axis_index("dp")
    held = epflat.shape[0] // PLEN
    all_rows = allq.shape[0]
    gathered = all_rows // QLEN
    embedding_dimension = groups * held
    dots = jnp.dot(allq, epflat.T, preferred_element_type=jnp.float32)
    expo = jnp.exp(dots / TAU).reshape(all_rows, held, PLEN)
    total = jnp.sum(expo, axis=2)
    similarity_logits = jnp.sum((TAU * jnp.log(total)).reshape(gathered, QLEN, held), axis=1)
    table = lax.dynamic_update_slice(
        jnp.zeros((gathered, embedding_dimension), jnp.float32),
        similarity_logits,
        (jnp.int32(0), here * held),
    )
    mine = lax.psum_scatter(table, "dp", scatter_dimension=0, tiled=True)
    place = negatives // held // lax.axis_size("mp") * held + negatives % held
    onehot = (
        place[:, :, None] == jnp.arange(embedding_dimension, dtype=jnp.int32)[None, None, :]
    ).astype(jnp.float32)
    student = jnp.sum(onehot * mine[:, None, :], axis=2)
    expo_s = jnp.exp(student)
    prob = expo_s / jnp.sum(expo_s, axis=1, keepdims=True)
    teach = jnp.exp(-ranks.astype(jnp.float32) / RANK_TEMP)
    teach = teach / jnp.sum(teach, axis=1, keepdims=True)
    dscore = prob - teach
    dcol = jnp.sum(onehot * dscore[:, :, None], axis=1)
    every = lax.all_gather(dcol, "dp", axis=0, tiled=True)
    owned = lax.dynamic_slice_in_dim(every, here * held, held, 1)
    share = jnp.repeat(owned, QLEN, axis=0) / total
    mixed = (expo * share[:, :, None]).reshape(all_rows, held * PLEN).astype(jnp.bfloat16)
    dep = jnp.dot(mixed.T, allq, preferred_element_type=jnp.float32)
    deq_all = jnp.dot(mixed, epflat, preferred_element_type=jnp.float32)
    deq = lax.psum_scatter(
        deq_all.astype(jnp.bfloat16), "dp", scatter_dimension=0, tiled=True
    ).astype(jnp.float32)
    dvq = (rq * (deq - eq * jnp.sum(eq * deq, axis=-1, keepdims=True))).astype(jnp.bfloat16)
    dvp = (rp * (dep - ep * jnp.sum(ep * dep, axis=-1, keepdims=True))).astype(jnp.bfloat16)
    grad_queries = jnp.dot(dvq, weight.T, preferred_element_type=jnp.float32).astype(jnp.bfloat16)
    local_grad = jnp.dot(query_states.T, dvq, preferred_element_type=jnp.float32) + jnp.dot(
        passage_states.T, dvp, preferred_element_type=jnp.float32
    )
    shares = lax.psum_scatter(local_grad, "mp", scatter_dimension=0, tiled=True)
    grad_weight = lax.psum(shares, "dp")
    return (grad_queries, grad_weight)


def solution(mesh):
    placed = (
        P(("dp", "mp"), None),
        P(("dp", "mp"), None),
        P("mp", None),
        P(("dp", "mp"), None),
        P(("dp", "mp"), None),
    )
    return jax.shard_map(
        on_device,
        mesh=mesh,
        in_specs=placed,
        out_specs=(P(("dp", "mp"), None), P("mp", None)),
        check_vma=False,
    )
```

profile of v0, /device:TPU:6, one launch (start us, length us, event | category | flops | bytes accessed | tf_op | source)
XLA Modules:
  0.0 460.7 jit_solution(670592779153172635)
XLA Ops:
  7.2 0.0 copy-start
  7.2 0.0 reduce-scatter.7.cloned.1.call-start
  7.2 0.9 fusion.12
  8.2 0.7 fusion.9
  8.9 44.9 %all_gather.9 = bf16[1024,128]{1,0:T(8,128)(2,1)S(1)} all-gather(bf16[16,128]{1,0:T(8,128)(2,1)} %param.7), channel_id=1, replica_groups=mesh['dp'=12,'mp'=64] {'mp'}, dimensions={0}, use_global_device_ids=true | all-gather | bytes 266240 | tf_op jit(solution)/shard_map/all_gather | solution.py:21
  53.8 1.2 multiply_reduce_fusion.2
  55.0 0.0 copy-start.7
  55.1 28.4 %all_gather.10 = bf16[1536,128]{0,1:T(8,128)(2,1)S(1)} all-gather(bf16[128,128]{0,1:T(8,128)(2,1)S(1)} %multiply_convert_fusion.4), channel_id=1, replica_groups=mesh['dp'=12,'mp'=64] {'dp'}, dimensions={0}, use_global_device_ids=true | all-gather | bytes 425984 | tf_op jit(solution)/shard_map/all_gather | solution.py:26
  83.5 0.0 copy-done
  83.5 0.0 copy-start.2
  83.5 1.0 multiply_reduce_fusion.1
  84.5 0.0 copy-start.1
  84.5 0.0 copy-done.2
  84.6 0.8 copy-done.1
  85.4 4.8 %fusion = f32[1536,1440]{0,1:T(8,128)} fusion(bf16[1536,128]{0,1:T(8,128)(2,1)S(1)} %all_gather.10, f32[1440,128]{1,0:T(8,128)S(1)} %get-tuple-element.13, f32[1440]{0:T(1024)S(1)} %add_rsqrt_fusion), kind=kOutput, calls=%fused_computation.2 | convolution fusion | flops 568811520 | bytes 9983616 | tf_op jit(solution)/shard_map/dot_general | solution.py:33
  90.2 0.0 copy-done.7
  90.2 7.6 %reshape.43 = f32[1536,8,180]{0,2,1:T(8,128)} reshape(f32[1536,1440]{0,1:T(8,128)} %fusion) | data formatting | bytes 17694720 | tf_op jit(solution)/shard_map/reshape | solution.py:34
  97.8 0.0 copy-start.6
  97.8 4.4 reduce_sum.92
  102.2 0.6 log_multiply_fusion
  102.8 0.9 mul.110
  103.7 0.1 reduce_sum.93
  103.8 0.1 copy.16
  103.9 0.3 dynamic_update_slice.3
  104.2 39.9 %all-reduce = f32[48,96]{1,0:T(8,128)S(1)} all-reduce(f32[48,96]{1,0:T(8,128)S(1)} %dynamic_update_slice.3), channel_id=2, replica_groups=mesh['dp'=12,'mp'=64] {'dp'}, use_global_device_ids=true, to_apply=%region_4.0.clone | all-reduce | flops 4608 | bytes 36864
  144.1 1.3 dynamic-slice
  146.0 0.2 select_reduce_fusion.1
  146.2 0.1 exponential_reduce_fusion
  146.3 0.0 copy-done.6
  146.3 0.1 divide_subtract_fusion
  146.4 0.1 select_reduce_fusion
  146.5 20.4 %all-gather = f32[12,4,96]{2,1,0:T(4,128)S(1)} all-gather(f32[1,4,96]{2,1,0:T(4,128)S(1)} %bitcast.29), channel_id=1, replica_groups=mesh['dp'=12,'mp'=64] {'dp'}, dimensions={0}, use_global_device_ids=true | all-gather | bytes 19968 | tf_op jit(solution)/shard_map/all_gather | solution.py:54
  167.0 0.1 constant_dynamic-slice_fusion.1
  167.0 0.1 copy.17
  167.1 0.1 broadcast_in_dim.5
  167.2 0.7 reshape.44
  168.0 0.8 div.73
  168.8 4.6 %mul.116 = f32[1536,8,180]{0,2,1:T(8,128)} broadcast(f32[1536,8]{0,1:T(8,128)S(1)} %div.73), dimensions={0,1} | broadcast | bytes 8896512 | tf_op jit(solution)/shard_map/mul | solution.py:57
  173.4 7.5 %mul.117 = f32[1536,1440]{0,1:T(8,128)} reshape(f32[1536,8,180]{0,2,1:T(8,128)} %mul.116) | data formatting | bytes 17694720 | tf_op jit(solution)/shard_map/mul | solution.py:57
  180.9 9.5 %multiply_convert_fusion = bf16[1536,1440]{0,1:T(8,128)(2,1)} fusion(f32[1536,1440]{0,1:T(8,128)} %fusion, f32[1536,1440]{0,1:T(8,128)} %mul.117), kind=kLoop, calls=%fused_computation.1 | loop fusion | flops 4423680 | bytes 22118400 | tf_op jit(solution)/shard_map/convert_element_type | solution.py:57
  190.4 4.9 %convolution_convert_fusion = bf16[1536,128]{1,0:T(8,128)(2,1)} fusion(bf16[1536,1440]{0,1:T(8,128)(2,1)} %multiply_convert_fusion, f32[1440,128]{1,0:T(8,128)} %copy-done.1, f32[1440]{0:T(1024)S(1)} %add_rsqrt_fusion), kind=kOutput, calls=%fused_computation.3 | convolution fusion | flops 566796288 | bytes 5559936 | tf_op jit(solution)/shard_map/dot_general | solution.py:59
  195.3 0.0 reduce-scatter.7.cloned.1.call-update
  195.4 0.0 copy-start.3
  195.4 0.2 reduce-scatter.9.cloned.1.call-start
  195.6 4.7 %multiply_reduce_fusion = (f32[1440]{0:T(1024)S(1)}, f32[1440,128]{1,0:T(8,128)}) fusion(f32[1440,128]{1,0:T(8,128)} %copy-done.1, f32[1440]{0:T(1024)S(1)} %add_rsqrt_fusion, bf16[1536,1440]{0,1:T(8,128)(2,1)} %multiply_convert_fusion, bf16[1536,128]{0,1:T(8,128)(2,1)} %copy-done.2), kind=kOutput, calls=%fused_computation.8 | convolution fusion | flops 566782592 | bytes 6302976 | tf_op jit(solution)/shard_map/dot_general | solution.py:58
  200.3 45.4 %reduce-scatter.7.cloned.1.call-done = bf16[128,128]{1,0:T(8,128)(2,1)} async-done(((bf16[1536,128]{1,0:T(8,128)(2,1)}), bf16[128,128]{1,0:T(8,128)(2,1)}) %reduce-scatter.7.cloned.1.call-update) | async-done | bytes 32784
  245.7 1.5 copy.21
  247.2 0.8 fusion.4
  248.0 0.8 fusion.6
  248.8 0.0 copy-done.3
  248.8 0.0 copy-start.4
  248.8 0.2 fusion.13
  249.0 0.4 copy-done.4
  249.4 0.0 copy-start.5
  249.4 3.5 fusion.1
  252.9 2.1 copy.22
  254.9 0.0 reduce-scatter.9.cloned.1.call-update
  255.0 0.0 copy-done.5
  255.0 1.0 convolution_convert_fusion.1
  255.9 151.4 %reduce-scatter.9.cloned.1.call-done = f32[16,128]{1,0:T(8,128)} async-done(((f32[1024,128]{1,0:T(8,128)}), f32[16,128]{1,0:T(8,128)}) %reduce-scatter.9.cloned.1.call-update) | async-done | bytes 8208
  407.3 0.8 copy.23
  408.1 45.1 %psum.7 = f32[16,128]{0,1:T(8,128)S(1)} all-reduce(f32[16,128]{0,1:T(8,128)S(1)} %copy.23), channel_id=1, replica_groups=mesh['dp'=12,'mp'=64] {'dp'}, use_global_device_ids=true, to_apply=%region_13.14 | all-reduce | flops 2048 | bytes 16384 | tf_op jit(solution)/shard_map/psum | solution.py:70
  453.2 0.7 copy.19
  (5 shorter events, 0.0 us)
Async XLA Ops:
  7.2 76.3 %copy-start = (bf16[1440,1024]{1,0:T(8,128)(2,1)S(1)}, bf16[1440,1024]{1,0:T(8,128)(2,1)}, u32[]{:S(2)}) copy-start(bf16[1440,1024]{1,0:T(8,128)(2,1)} %param.6) | copy-start | bytes 8847364
  7.2 238.6 %reduce-scatter.7.cloned.1.call-start = ((), (), s32[]{:S(2)}) async-start(), calls=%async_computation.2 | async-start | bytes 425984
  55.0 35.2 %copy-start.7 = (f32[128]{0:T(128)}, f32[128]{0:T(128)S(1)}, u32[]{:S(2)}) copy-start(f32[128]{0:T(128)S(1)} %add_rsqrt_fusion.1) | copy-start | bytes 1540
  83.5 1.1 copy-start.2
  84.5 0.9 copy-start.1
  97.8 48.5 %copy-start.6 = (s32[4,32]{1,0:T(4,128)S(1)}, s32[4,32]{1,0:T(4,128)}, u32[]{:S(2)}) copy-start(s32[4,32]{1,0:T(4,128)} %param.9) | copy-start | bytes 1540
  195.4 53.4 %copy-start.3 = (bf16[128,1024]{1,0:T(8,128)(2,1)S(1)}, bf16[128,1024]{1,0:T(8,128)(2,1)}, u32[]{:S(2)}) copy-start(bf16[128,1024]{1,0:T(8,128)(2,1)} %param.5) | copy-start | bytes 786436
  195.4 211.9 %reduce-scatter.9.cloned.1.call-start = ((), (), s32[]{:S(2)}) async-start(), calls=%async_computation.3 | async-start | bytes 532480
  248.8 0.6 copy-start.4
  249.4 5.5 %copy-start.5 = (bf16[128,128]{0,1:T(8,128)(2,1)S(1)}, bf16[128,128]{0,1:T(8,128)(2,1)}, u32[]{:S(2)}) copy-start(bf16[128,128]{0,1:T(8,128)(2,1)} %copy-done.4) | copy-start | bytes 98308
Sparse Core Ops, SparseCore 0:
  195.5 50.2 reduce-scatter.6
  255.1 152.1 reduce-scatter.8
where the time goes:
time: 462 us; the launch traced here: 461 us
  waiting for transfers between devices  197 us (43%)
  blocking collectives  179 us (39%)
  local copies, waits for them, and re-layouts  29.5 us (6%)
  matrix products  21.4 us (5%)
  other arithmetic  19.2 us (4%)
  between operations  14.9 us (3%)
    unnamed x4, waiting for transfers between devices  197 us
    psum x1, blocking collectives, on_device(): grad_weight = lax.psum(shares, 'dp')  45.1 us
    all_gather x1, blocking collectives, on_device(): weight = lax.all_gather(proj_weight, 'mp', axis=0, tiled=True)  44.9 us
    unnamed x1, blocking collectives  39.9 us
    all_gather x1, blocking collectives, on_device(): allq = lax.all_gather(eqb, 'dp', axis=0, tiled=True)  28.4 us
    all_gather x1, blocking collectives, on_device(): every = lax.all_gather(dcol, 'dp', axis=0, tiled=True)  20.4 us
    mul x2, local copies, waits for them, and re-layouts, on_device(): expo * share[:, :, None]  12.1 us
    convert_element_type x1, other arithmetic, on_device(): (expo * share[:, :, None]).reshape(all_rows, held * PLEN)  9.51 us
  transfers between devices with their start and end apart: 2, of which 2 were waited for; matrix products, arithmetic and copies ran while one was open for 1% of the time, Pallas kernels for 0%

commit v1 on v0

v1 whole, which is shorter than its diff:
```python
import functools

import jax
import jax.numpy as jnp
from jax import lax
from jax.experimental import pallas as pl
from jax.experimental.pallas import tpu as pltpu
from jax.sharding import Mesh
from jax.sharding import PartitionSpec as P

QLEN = 32
PLEN = 180
PROWS = 192
TAU = 0.1
RANK_TEMP = 8.0
EPS = 1e-06
LOG2E = 1.4426950408889634
F32 = jnp.float32
BF16 = jnp.bfloat16
MP = ("x", "y", "core")
ALL = ("dp", "x", "y", "core")


def contract(a, b, dims):
    return lax.dot_general(a, b, (dims, ((), ())), preferred_element_type=F32)


def lanes(shape):
    return lax.broadcasted_iota(jnp.int32, shape, 1)


def query_sums(x):
    width = x.shape[1]
    for s in (1, 2, 4, 8, 16):
        x = x + pltpu.roll(x, s, 1)
    x = jnp.where(lanes(x.shape) % QLEN == QLEN - 1, x, 0.0)
    for s in (1, 2, 4, 8, 16):
        x = x + pltpu.roll(x, width - s, 1)
    return x


def query_kernel(dp, n_mp, hq_ref, w_ref, neg_ref, rank_ref, tx_ref, vt_ref):
    held = 8
    vt = jnp.dot(hq_ref[...], w_ref[...], preferred_element_type=F32).T
    vt_ref[...] = vt
    et = vt * lax.rsqrt(jnp.sum(vt * vt, axis=0, keepdims=True) + EPS)
    etb = et.astype(BF16)
    neg = neg_ref[...]
    place = lax.div(neg, held * n_mp) * held + lax.rem(neg, held)
    teach = jnp.exp(-rank_ref[...].astype(F32) / RANK_TEMP)
    teach = teach / jnp.sum(teach, axis=1, keepdims=True)
    slots = dp * held
    row = lax.broadcasted_iota(jnp.int32, (slots, neg.shape[1]), 0)
    lane = lanes((slots, 128))
    table = jnp.zeros((slots, 128), F32)
    for q in range(neg.shape[0]):
        mine = jnp.where(place[q : q + 1, :] == row, teach[q : q + 1, :], 0.0)
        column = jnp.sum(mine, axis=1, keepdims=True)
        table = jnp.where(lane // QLEN == q, column, table)
    high = table.astype(BF16).astype(F32)
    low = table - high
    for d in range(dp):
        tx_ref[d, 0:128, :] = etb
        cut = slice(held * d, held * d + held)
        tx_ref[d, 128:144, :] = jnp.concatenate([high[cut], low[cut]], axis=0).astype(BF16)


def score_kernel(dp, hp_ref, w_ref, rx_ref, tx_ref, v_ref, expo_ref, sa_ref, sb_ref, ef, eb, lhs, sums):
    held = 8
    v_ref[...] = jnp.dot(hp_ref[...], w_ref[...], preferred_element_type=F32)
    row = lax.broadcasted_iota(jnp.int32, (16, PROWS), 0)
    col = lanes((16, PROWS))
    for p in range(held):
        v = v_ref[PLEN * p : PLEN * (p + 1), :]
        e = v * lax.rsqrt(jnp.sum(v * v, axis=1, keepdims=True) + EPS)
        ef[p, 176:256, :] = jnp.zeros((80, 128), F32)
        ef[p, 0:PLEN, :] = e
        padded = ef[p]
        eb[PROWS * p : PROWS * (p + 1), :] = padded[0:PROWS].astype(BF16)
        lhs[p, 0:128, :] = padded.T[:, 0:PROWS].astype(BF16)
        lhs[p, 128:144, :] = jnp.where((row == p) & (col < PLEN), 1.0, 0.0).astype(BF16)
    sums[...] = jnp.zeros((16, 128), F32)
    for j in range(dp // 2):
        pair = (2 * j, 2 * j + 1)
        wide = slice(256 * j, 256 * (j + 1))
        q = jnp.concatenate([rx_ref[k, 0:128, :] for k in pair], axis=1)
        codes = jnp.concatenate([rx_ref[k, 128:144, :].astype(F32) for k in pair], axis=1)
        teach = codes[0:8] + codes[8:16]
        listed = teach > 0.0
        dots = jnp.dot(eb[...], q, preferred_element_type=F32)
        expo = jnp.exp2(dots * (LOG2E / TAU)).astype(BF16)
        expo_ref[:, wide] = expo
        near = []
        total = None
        for p in range(held):
            out = jnp.dot(lhs[p], expo[PROWS * p : PROWS * (p + 1)], preferred_element_type=F32)
            near.append(out[0:128])
            total = out[128:136] if p == 0 else total + out[128:136]
        score = query_sums(TAU * jnp.log(total))
        es = jnp.where(listed, jnp.exp(score), 0.0)
        sa = es / total
        sb = teach / total
        sa_ref[:, wide] = sa
        sb_ref[:, wide] = sb
        a = near[0] * sa[0:1]
        b = near[0] * sb[0:1]
        for p in range(1, held):
            a = a + near[p] * sa[p : p + 1]
            b = b + near[p] * sb[p : p + 1]
        ab, bb = a.astype(BF16), b.astype(BF16)
        part = jnp.sum(es, axis=0, keepdims=True)
        for h, k in enumerate(pair):
            cut = slice(128 * h, 128 * (h + 1))
            tx_ref[k, 0:128, :] = ab[:, cut]
            tx_ref[k, 128:256, :] = bb[:, cut]
            sums[k : k + 1, :] = part[:, cut]
    whole = sums[...]
    high = whole.astype(BF16).astype(F32)
    rest = whole - high
    mid = rest.astype(BF16).astype(F32)
    low = rest - mid
    at = lanes((16, 128)) % QLEN
    coded = jnp.where(at == 0, high, jnp.where(at == 1, mid, jnp.where(at == 2, low, 0.0)))
    row16 = lax.broadcasted_iota(jnp.int32, (16, 128), 0)
    for d in range(dp):
        tx_ref[d, 256:272, :] = jnp.where(row16 == dp, coded[d : d + 1], coded).astype(BF16)


def grad_kernel(dp, hq_ref, hp_ref, w_ref, rx2_ref, rx_ref, vt_ref, v_ref, expo_ref, sa_ref, sb_ref, gq_ref, gw_ref, dv):
    held = 8
    part = rx_ref[0, 256:272, :].astype(F32)
    a = rx_ref[0, 0:128, :].astype(F32)
    b = rx_ref[0, 128:256, :].astype(F32)
    for s in range(1, dp):
        part = part + rx_ref[s, 256:272, :].astype(F32)
        a = a + rx_ref[s, 0:128, :].astype(F32)
        b = b + rx_ref[s, 128:256, :].astype(F32)
    sums = query_sums(part)
    inv = 1.0 / jnp.where(sums > 0.0, sums, 1.0)
    deq = a * inv[dp : dp + 1] - b
    vt = vt_ref[...]
    r = lax.rsqrt(jnp.sum(vt * vt, axis=0, keepdims=True) + EPS)
    et = vt * r
    dvq = (r * (deq - et * jnp.sum(et * deq, axis=0, keepdims=True))).astype(BF16)
    gq_ref[...] = contract(dvq, w_ref[...], ((0,), (1,))).astype(BF16)
    qt = jnp.concatenate([rx2_ref[k, 0:128, :] for k in range(dp)], axis=1).astype(F32)
    wide_inv = jnp.concatenate([inv[k : k + 1] for k in range(dp)], axis=1)
    share = sa_ref[...] * wide_inv - sb_ref[...]
    for p in range(held):
        scaled = (qt * share[p : p + 1]).astype(BF16)
        dep = contract(expo_ref[PROWS * p : PROWS * (p + 1), :], scaled, ((1,), (1,)))[0:PLEN]
        v = v_ref[PLEN * p : PLEN * (p + 1), :]
        rp = lax.rsqrt(jnp.sum(v * v, axis=1, keepdims=True) + EPS)
        e = v * rp
        dv[PLEN * p : PLEN * (p + 1), :] = rp * (dep - e * jnp.sum(e * dep, axis=1, keepdims=True))
    dvp = dv[...].astype(BF16)
    gwt = contract(dvp, hp_ref[...], ((0,), (0,))) + jnp.dot(dvq, hq_ref[...], preferred_element_type=F32)
    gw_ref[...] = gwt.T.astype(BF16)


def call(kernel, outs, scratch=()):
    return pl.pallas_call(
        kernel,
        out_shape=[jax.ShapeDtypeStruct(s, t) for s, t in outs],
        scratch_shapes=[pltpu.VMEM(s, t) for s, t in scratch],
        compiler_params=pltpu.CompilerParams(vmem_limit_bytes=48 * 1024 * 1024),
    )


def on_device(dp, n_mp, hq, hp, proj_weight, negatives, ranks):
    rows = proj_weight.shape[0]
    sent = jnp.broadcast_to(proj_weight[None], (n_mp,) + proj_weight.shape)
    weight = lax.all_to_all(sent, MP, 0, 0).reshape(n_mp * rows, 128)
    tx2, vt = call(
        functools.partial(query_kernel, dp, n_mp), [((dp, 144, 128), BF16), ((128, 128), F32)]
    )(hq, weight, negatives, ranks)
    rx2 = lax.all_to_all(tx2, "dp", 0, 0)
    n_q = dp * 128
    tx3, v, expo, sa, sb = call(
        functools.partial(score_kernel, dp),
        [
            ((dp, 272, 128), BF16),
            ((8 * PLEN, 128), F32),
            ((8 * PROWS, n_q), BF16),
            ((8, n_q), F32),
            ((8, n_q), F32),
        ],
        [((8, 256, 128), F32), ((8 * PROWS, 128), BF16), ((8, 144, PROWS), BF16), ((16, 128), F32)],
    )(hp, weight, rx2)
    rx3 = lax.all_to_all(tx3, "dp", 0, 0)
    grad_queries, gw = call(
        functools.partial(grad_kernel, dp),
        [((128, n_mp * rows), BF16), ((n_mp * rows, 128), BF16)],
        [((8 * PLEN, 128), F32)],
    )(hq, hp, weight, rx2, rx3, vt, v, expo, sa, sb)
    terms = lax.all_to_all(gw.reshape(n_mp, rows, 128), MP, 0, 0)
    mine = jnp.sum(terms.astype(F32), axis=0)
    shares = lax.all_to_all(jnp.broadcast_to(mine[None], (dp,) + mine.shape), "dp", 0, 0)
    return grad_queries, jnp.sum(shares, axis=0)


def solution(mesh):
    dp = mesh.shape["dp"]
    n_mp = mesh.shape["mp"]
    cut = (4, 8, 2) if n_mp == 64 else (n_mp, 1, 1)
    finer = Mesh(mesh.devices.reshape((dp,) + cut), ALL)
    placed = (P(ALL, None), P(ALL, None), P(MP, None), P(ALL, None), P(ALL, None))
    return jax.shard_map(
        functools.partial(on_device, dp, n_mp),
        mesh=finer,
        in_specs=placed,
        out_specs=(P(ALL, None), P(MP, None)),
        check_vma=False,
    )
```

time: 462 us -> 151 us (0.33)
  waiting for transfers between devices: 197 us -> 0 us
  blocking collectives: 179 us -> 130 us
  local copies, waits for them, and re-layouts: 29.5 us -> 4.88 us
  matrix products: 21.4 us -> 0 us
  other arithmetic: 19.2 us -> 0.68 us
  Pallas kernels: 0 us -> 14.9 us
  between operations: 14.9 us -> 0.67 us
    unnamed x4 -> x0, waiting for transfers between devices: 197 us -> none
    all_to_all x0 -> x5, blocking collectives: none -> 130 us  [the longest x1 37.6 us: on_device(): rx3 = lax.all_to_all(tx3, 'dp', 0, 0)]
    all_gather x3 -> x0, blocking collectives: 93.7 us -> none  [the longest x1 44.9 us: on_device(): weight = lax.all_gather(proj_weight, 'mp', axis=0, tiled=True)]
    psum x1 -> x0, blocking collectives: 45.1 us -> none  [on_device(): grad_weight = lax.psum(shares, 'dp')]
    unnamed x1 -> x0, blocking collectives: 39.9 us -> none
    dot_general x8 -> x0, matrix products: 21.4 us -> none  [the longest x1 4.9 us: on_device(): deq_all = jnp.dot(mixed, epflat, preferred_element_type=jnp.float32)]
    pallas_call x0 -> x3, Pallas kernels: none -> 14.9 us  [the longest x1 9.37 us: on_device(): call(functools.partial(score_kernel, dp), [((dp, 272, 128), BF16), ((8 *...]
    mul x3 -> x0, local copies, waits for them, and re-layouts: 13 us -> none  [the longest x2 12.1 us: on_device(): expo * share[:, :, None]]
  transfers between devices with their start and end apart: 2 -> 0, of which waited for: 2 -> 0; matrix products, arithmetic and copies ran while one was open for 1% -> 0% of each run, Pallas kernels for 0% -> 0%
where the time goes in v1:
time: 151 us
  blocking collectives  130 us (86%)
  Pallas kernels  14.9 us (10%)
  local copies, waits for them, and re-layouts  4.88 us (3%)
    all_to_all x1, blocking collectives, on_device(): rx3 = lax.all_to_all(tx3, 'dp', 0, 0)  37.6 us
    all_to_all x1, blocking collectives, on_device(): rx2 = lax.all_to_all(tx2, 'dp', 0, 0)  35.5 us
    all_to_all x1, blocking collectives, on_device(): weight = lax.all_to_all(sent, MP, 0, 0).reshape(n_mp * rows, 128)  24.6 us
    all_to_all x1, blocking collectives, on_device(): terms = lax.all_to_all(gw.reshape(n_mp, rows, 128), MP, 0, 0)  17.6 us
    all_to_all x1, blocking collectives, on_device(): lax.all_to_all(jnp.broadcast_to(mine[None], (dp,) + mine.shape), 'dp', 0, 0)  14.4 us
    pallas_call x1, Pallas kernels, on_device(): call(functools.partial(score_kernel, dp), [((dp, 272, 128), BF16), ((8 *...  9.37 us
    pallas_call x1, Pallas kernels, on_device(): call(functools.partial(grad_kernel, dp), [((128, n_mp * rows), BF16), ((n...  5.23 us
    unnamed x10, local copies, waits for them, and re-layouts  4.15 us

profile of v1, /device:TPU:6, one launch (start us, length us, event | category | flops | bytes accessed | tf_op | source)
XLA Modules:
  0.0 150.9 jit_solution(14399723603378817358)
XLA Ops:
  0.6 0.7 broadcast_in_dim.4
  1.4 24.6 %all_to_all.25 = bf16[64,16,128]{2,1,0:T(8,128)(2,1)S(1)} all-to-all(bf16[64,16,128]{2,1,0:T(8,128)(2,1)S(1)} %broadcast_in_dim.4), channel_id=1, replica_groups=mesh['dp'=12,'x'=4,'y'=8,'core'=2] {'x','y','core'}, dimensions={0} | all-to-all | bytes 524288 | tf_op jit(solution)/shard_map/all_to_all | solution.py:173
  26.0 0.0 copy-start.2
  26.0 0.9 copy-done.2
  26.9 0.0 copy-start.3
  26.9 0.7 copy-done.3
  27.6 0.0 copy-start.4
  27.6 0.7 copy-done.4
  28.3 0.3 shard_map.68
  28.6 35.5 %all_to_all.26.rx_ref.rx2_ref = bf16[12,144,128]{2,1,0:T(8,128)(2,1)S(1)} all-to-all(bf16[12,144,128]{2,1,0:T(8,128)(2,1)S(1)} %get-tuple-element.11), channel_id=1, replica_groups=mesh['dp'=12,'x'=4,'y'=8,'core'=2] {'dp'}, dimensions={0} | all-to-all | bytes 884736 | tf_op jit(solution)/shard_map/all_to_all | solution.py:177
  64.1 0.0 copy-start
  64.1 1.8 %copy-done = bf16[1440,1024]{1,0:T(8,128)(2,1)S(1)} copy-done((bf16[1440,1024]{1,0:T(8,128)(2,1)S(1)}, bf16[1440,1024]{1,0:T(8,128)(2,1)}, u32[]{:S(2)}) %copy-start) | copy-done | bytes 2949144
  65.9 0.0 copy-start.1
  65.9 9.4 %shard_map.69 = (bf16[12,272,128]{2,1,0:T(8,128)(2,1)S(1)}, f32[1440,128]{1,0:T(8,128)S(1)}, bf16[1536,1536]{1,0:T(8,128)(2,1)}, f32[8,1536]{1,0:T(8,128)S(1)}, f32[8,1536]{1,0:T(8,128)S(1)}) custom-call(bf16[1440,1024]{1,0:T(8,128)(2,1)S(1)} %copy-done, bf16[1024,128]{1,0:T(8,128)(2,1)S(1)} %bitcast.3, bf16[12,144,128]{2,1,0:T(8,128)(2,1)S(1)} %all_to_all.26.rx_ref.rx2_ref), custom_call_target="tpu_custom_call" | custom-call | tf_op jit(solution)/shard_map/pallas_call | solution.py:179
  75.3 37.6 %all_to_all.27.rx_ref = bf16[12,272,128]{2,1,0:T(8,128)(2,1)S(1)} all-to-all(bf16[12,272,128]{2,1,0:T(8,128)(2,1)S(1)} %get-tuple-element.12), channel_id=1, replica_groups=mesh['dp'=12,'x'=4,'y'=8,'core'=2] {'dp'}, dimensions={0} | all-to-all | bytes 1671168 | tf_op jit(solution)/shard_map/all_to_all | solution.py:190
  112.9 0.0 copy-done.1
  112.9 5.2 %shard_map.70 = (bf16[128,1024]{1,0:T(8,128)(2,1)}, bf16[1024,128]{1,0:T(8,128)(2,1)S(1)}) custom-call(bf16[128,1024]{1,0:T(8,128)(2,1)S(1)} %copy-done.2, bf16[1440,1024]{1,0:T(8,128)(2,1)S(1)} %copy-done.1, bf16[1024,128]{1,0:T(8,128)(2,1)S(1)} %bitcast.4, bf16[12,144,128]{2,1,0:T(8,128)(2,1)S(1)} %all_to_all.26.rx_ref.rx2_ref, ...), custom_call_target="tpu_custom_call" | custom-call | tf_op jit(solution)/shard_map/pallas_call | solution.py:191
  118.2 17.6 %all_to_all.28 = bf16[64,16,128]{2,1,0:T(8,128)(2,1)S(1)} all-to-all(bf16[64,16,128]{2,1,0:T(8,128)(2,1)S(1)} %bitcast.5), channel_id=1, replica_groups=mesh['dp'=12,'x'=4,'y'=8,'core'=2] {'x','y','core'}, dimensions={0} | all-to-all | bytes 524288 | tf_op jit(solution)/shard_map/all_to_all | solution.py:196
  135.8 0.1 convert_reduce_fusion
  135.9 14.4 %all_to_all.29 = f32[12,16,128]{2,1,0:T(8,128)S(1)} all-to-all(f32[12,16,128]{2,1,0:T(8,128)S(1)} %broadcast_in_dim.5), channel_id=1, replica_groups=mesh['dp'=12,'x'=4,'y'=8,'core'=2] {'dp'}, dimensions={0} | all-to-all | bytes 196608 | tf_op jit(solution)/shard_map/all_to_all | solution.py:198
  150.3 0.6 reduce_sum.19
  (1 shorter events, 0.0 us)
Async XLA Ops:
  26.0 1.0 copy-start.2
  26.9 0.7 copy-start.3
  27.6 0.7 copy-start.4
  64.1 1.8 %copy-start = (bf16[1440,1024]{1,0:T(8,128)(2,1)S(1)}, bf16[1440,1024]{1,0:T(8,128)(2,1)}, u32[]{:S(2)}) copy-start(bf16[1440,1024]{1,0:T(8,128)(2,1)} %hp_ref.3) | copy-start | bytes 8847364
  65.9 47.0 %copy-start.1 = (bf16[1440,1024]{1,0:T(8,128)(2,1)S(1)}, bf16[1440,1024]{1,0:T(8,128)(2,1)}, u32[]{:S(2)}) copy-start(bf16[1440,1024]{1,0:T(8,128)(2,1)} %hp_ref.3) | copy-start | bytes 8847364

commit v2 on v1

v2 whole, which is shorter than its diff:
```python
import functools

import jax
import jax.numpy as jnp
from jax import lax
from jax.experimental import pallas as pl
from jax.experimental.pallas import tpu as pltpu
from jax.sharding import Mesh
from jax.sharding import PartitionSpec as P

QLEN = 32
PLEN = 180
PROWS = 192
TAU = 0.1
RANK_TEMP = 8.0
EPS = 1e-06
LOG2E = 1.4426950408889634
F32 = jnp.float32
BF16 = jnp.bfloat16
MP = ("x", "y", "core")
ALL = ("dp", "x", "y", "core")


def contract(a, b, dims):
    return lax.dot_general(a, b, (dims, ((), ())), preferred_element_type=F32)


def lanes(shape):
    return lax.broadcasted_iota(jnp.int32, shape, 1)


def query_sums(x):
    width = x.shape[1]
    for s in (1, 2, 4, 8, 16):
        x = x + pltpu.roll(x, s, 1)
    x = jnp.where(lanes(x.shape) % QLEN == QLEN - 1, x, 0.0)
    for s in (1, 2, 4, 8, 16):
        x = x + pltpu.roll(x, width - s, 1)
    return x


def query_kernel(dp, n_mp, hq_hbm, w_ref, neg_hbm, rank_hbm, tx_ref, vt_ref, hq, neg_ref, rank_ref, sems):
    held = 8
    copies = [
        pltpu.make_async_copy(src, dst, sems.at[i])
        for i, (src, dst) in enumerate(((neg_hbm, neg_ref), (rank_hbm, rank_ref), (hq_hbm, hq)))
    ]
    for copy in copies:
        copy.start()
    copies[0].wait()
    copies[1].wait()
    neg = neg_ref[...]
    place = lax.div(neg, held * n_mp) * held + lax.rem(neg, held)
    teach = jnp.exp(-rank_ref[...].astype(F32) / RANK_TEMP)
    teach = teach / jnp.sum(teach, axis=1, keepdims=True)
    slots = dp * held
    row = lax.broadcasted_iota(jnp.int32, (slots, neg.shape[1]), 0)
    lane = lanes((slots, 128))
    table = jnp.zeros((slots, 128), F32)
    for q in range(neg.shape[0]):
        mine = jnp.where(place[q : q + 1, :] == row, teach[q : q + 1, :], 0.0)
        column = jnp.sum(mine, axis=1, keepdims=True)
        table = jnp.where(lane // QLEN == q, column, table)
    high = table.astype(BF16).astype(F32)
    low = table - high
    for d in range(dp):
        cut = slice(held * d, held * d + held)
        tx_ref[d, 128:144, :] = jnp.concatenate([high[cut], low[cut]], axis=0).astype(BF16)
    copies[2].wait()
    vt = jnp.dot(hq[...], w_ref[...], preferred_element_type=F32).T
    vt_ref[...] = vt
    et = vt * lax.rsqrt(jnp.sum(vt * vt, axis=0, keepdims=True) + EPS)
    etb = et.astype(BF16)
    for d in range(dp):
        tx_ref[d, 0:128, :] = etb


def score_kernel(
    dp, hp_hbm, w_ref, rx_ref, tx_ref, v_ref, expo_ref, sa_ref, sb_ref, a_ref, b_ref, hp, ef, eb, lhs, sums, sems
):
    held = 8
    parts = 3
    chunk = held * PLEN // parts
    copies = [
        pltpu.make_async_copy(
            hp_hbm.at[pl.ds(chunk * i, chunk)], hp.at[pl.ds(chunk * i, chunk)], sems.at[i]
        )
        for i in range(parts)
    ]
    for copy in copies:
        copy.start()
    row = lax.broadcasted_iota(jnp.int32, (16, PROWS), 0)
    col = lanes((16, PROWS))
    for p in range(held):
        lhs[p, 128:144, :] = jnp.where((row == p) & (col < PLEN), 1.0, 0.0).astype(BF16)
        ef[p, 176:256, :] = jnp.zeros((80, 128), F32)
    sums[...] = jnp.zeros((16, 128), F32)
    for i in range(parts):
        cut = slice(chunk * i, chunk * (i + 1))
        copies[i].wait()
        v_ref[cut, :] = jnp.dot(hp[cut, :], w_ref[...], preferred_element_type=F32)
    for p in range(held):
        v = v_ref[PLEN * p : PLEN * (p + 1), :]
        ef[p, 0:PLEN, :] = v * lax.rsqrt(jnp.sum(v * v, axis=1, keepdims=True) + EPS)
        padded = ef[p]
        eb[PROWS * p : PROWS * (p + 1), :] = padded[0:PROWS].astype(BF16)
        lhs[p, 0:128, :] = padded.T[:, 0:PROWS].astype(BF16)
    for j in range(dp // 2):
        pair = (2 * j, 2 * j + 1)
        wide = slice(256 * j, 256 * (j + 1))
        q = jnp.concatenate([rx_ref[k, 0:128, :] for k in pair], axis=1)
        codes = jnp.concatenate([rx_ref[k, 128:144, :].astype(F32) for k in pair], axis=1)
        teach = codes[0:8] + codes[8:16]
        listed = teach > 0.0
        dots = jnp.dot(eb[...], q, preferred_element_type=F32)
        expo = jnp.exp2(dots * (LOG2E / TAU)).astype(BF16)
        expo_ref[:, wide] = expo
        near = []
        total = None
        for p in range(held):
            out = jnp.dot(lhs[p], expo[PROWS * p : PROWS * (p + 1)], preferred_element_type=F32)
            near.append(out[0:128])
            total = out[128:136] if p == 0 else total + out[128:136]
        score = query_sums(TAU * jnp.log(total))
        es = jnp.where(listed, jnp.exp(score), 0.0)
        sa = es / total
        sb = teach / total
        sa_ref[:, wide] = sa
        sb_ref[:, wide] = sb
        a = near[0] * sa[0:1]
        b = near[0] * sb[0:1]
        for p in range(1, held):
            a = a + near[p] * sa[p : p + 1]
            b = b + near[p] * sb[p : p + 1]
        a_ref[:, wide] = a
        b_ref[:, wide] = b
        part = jnp.sum(es, axis=0, keepdims=True)
        for h, k in enumerate(pair):
            sums[k : k + 1, :] = part[:, 128 * h : 128 * (h + 1)]
    whole = sums[...]
    high = whole.astype(BF16).astype(F32)
    rest = whole - high
    mid = rest.astype(BF16).astype(F32)
    low = rest - mid
    at = lanes((16, 128)) % QLEN
    coded = jnp.where(at == 0, high, jnp.where(at == 1, mid, jnp.where(at == 2, low, 0.0)))
    for d in range(dp):
        tx_ref[d] = coded.astype(BF16)


def passage_kernel(dp, rx2_ref, rx_ref, v_ref, expo_ref, sa_ref, sb_ref, a_ref, b_ref, tx_ref, dv_ref, dv):
    held = 8
    part = rx_ref[0].astype(F32)
    for s in range(1, dp):
        part = part + rx_ref[s].astype(F32)
    sums = query_sums(part)
    inv = 1.0 / jnp.where(sums > 0.0, sums, 1.0)
    for k in range(dp):
        cut = slice(128 * k, 128 * (k + 1))
        tx_ref[k] = (a_ref[:, cut] * inv[k : k + 1] - b_ref[:, cut]).astype(BF16)
    qt = jnp.concatenate([rx2_ref[k, 0:128, :] for k in range(dp)], axis=1).astype(F32)
    wide_inv = jnp.concatenate([inv[k : k + 1] for k in range(dp)], axis=1)
    share = sa_ref[...] * wide_inv - sb_ref[...]
    for p in range(held):
        scaled = (qt * share[p : p + 1]).astype(BF16)
        dep = contract(expo_ref[PROWS * p : PROWS * (p + 1), :], scaled, ((1,), (1,)))[0:PLEN]
        v = v_ref[PLEN * p : PLEN * (p + 1), :]
        rp = lax.rsqrt(jnp.sum(v * v, axis=1, keepdims=True) + EPS)
        e = v * rp
        dv[PLEN * p : PLEN * (p + 1), :] = rp * (dep - e * jnp.sum(e * dep, axis=1, keepdims=True))
    dv_ref[...] = dv[...].astype(BF16)


def grad_kernel(dp, hq_ref, hp_ref, w_ref, rx_ref, vt_ref, dvp_ref, gq_ref, gw_ref):
    deq = rx_ref[0].astype(F32)
    for s in range(1, dp):
        deq = deq + rx_ref[s].astype(F32)
    vt = vt_ref[...]
    r = lax.rsqrt(jnp.sum(vt * vt, axis=0, keepdims=True) + EPS)
    et = vt * r
    dvq = (r * (deq - et * jnp.sum(et * deq, axis=0, keepdims=True))).astype(BF16)
    gq_ref[...] = contract(dvq, w_ref[...], ((0,), (1,))).astype(BF16)
    gwt = contract(dvp_ref[...], hp_ref[...], ((0,), (0,)))
    gwt = gwt + jnp.dot(dvq, hq_ref[...], preferred_element_type=F32)
    gw_ref[...] = gwt.T.astype(BF16)


def call(kernel, outs, scratch=(), far=(), n_in=0, mib=20):
    specs = [pl.BlockSpec(memory_space=pltpu.HBM if i in far else pltpu.VMEM) for i in range(n_in)]
    return pl.pallas_call(
        kernel,
        out_shape=[jax.ShapeDtypeStruct(s, t) for s, t in outs],
        in_specs=specs,
        scratch_shapes=[pltpu.VMEM(*s) if isinstance(s, tuple) else s for s in scratch],
        compiler_params=pltpu.CompilerParams(vmem_limit_bytes=mib * 1024 * 1024),
    )


def on_device(dp, n_mp, hq, hp, proj_weight, negatives, ranks):
    rows = proj_weight.shape[0]
    width = n_mp * rows
    n_q = dp * 128
    n_p = 8 * PLEN
    sent = jnp.broadcast_to(proj_weight[None], (n_mp,) + proj_weight.shape)
    weight = lax.all_to_all(sent, MP, 0, 0).reshape(width, 128)
    tx2, vt = call(
        functools.partial(query_kernel, dp, n_mp),
        [((dp, 144, 128), BF16), ((128, 128), F32)],
        [
            (hq.shape, BF16),
            (negatives.shape, jnp.int32),
            (ranks.shape, jnp.int32),
            pltpu.SemaphoreType.DMA((3,)),
        ],
        far=(0, 2, 3),
        n_in=4,
    )(hq, weight, negatives, ranks)
    rx2 = lax.all_to_all(tx2, "dp", 0, 0)
    tx3, v, expo, sa, sb, a, b = call(
        functools.partial(score_kernel, dp),
        [
            ((dp, 16, 128), BF16),
            ((n_p, 128), F32),
            ((8 * PROWS, n_q), BF16),
            ((8, n_q), F32),
            ((8, n_q), F32),
            ((128, n_q), F32),
            ((128, n_q), F32),
        ],
        [
            (hp.shape, BF16),
            ((8, 256, 128), F32),
            ((8 * PROWS, 128), BF16),
            ((8, 144, PROWS), BF16),
            ((16, 128), F32),
            pltpu.SemaphoreType.DMA((3,)),
        ],
        far=(0,),
        n_in=3,
    )(hp, weight, rx2)
    rx3 = lax.all_to_all(tx3, "dp", 0, 0)
    tx4, dvp = call(
        functools.partial(passage_kernel, dp),
        [((dp, 128, 128), BF16), ((n_p, 128), BF16)],
        [((n_p, 128), F32)],
        n_in=8,
    )(rx2, rx3, v, expo, sa, sb, a, b)
    rx4 = lax.all_to_all(tx4, "dp", 0, 0)
    grad_queries, gw = call(
        functools.partial(grad_kernel, dp), [((128, width), BF16), ((width, 128), BF16)], n_in=6
    )(hq, hp, weight, rx4, vt, dvp)
    terms = lax.all_to_all(gw.reshape(n_mp, rows, 128), MP, 0, 0)
    mine = jnp.sum(terms.astype(F32), axis=0)
    shares = lax.all_to_all(jnp.broadcast_to(mine[None], (dp,) + mine.shape), "dp", 0, 0)
    return grad_queries, jnp.sum(shares, axis=0)


def solution(mesh):
    dp = mesh.shape["dp"]
    n_mp = mesh.shape["mp"]
    cut = (4, 8, 2) if n_mp == 64 else (n_mp, 1, 1)
    finer = Mesh(mesh.devices.reshape((dp,) + cut), ALL)
    placed = (P(ALL, None), P(ALL, None), P(MP, None), P(ALL, None), P(ALL, None))
    return jax.shard_map(
        functools.partial(on_device, dp, n_mp),
        mesh=finer,
        in_specs=placed,
        out_specs=(P(ALL, None), P(MP, None)),
        check_vma=False,
    )
```

time: 151 us -> 146 us (0.967)
  blocking collectives: 130 us -> 127 us
  Pallas kernels: 14.9 us -> 12 us
    all_to_all x1, blocking collectives: 37.6 us -> 13.6 us  [on_device(): rx3 = lax.all_to_all(tx3, 'dp', 0, 0)]
    all_to_all x1 -> x2, blocking collectives: 24.6 us -> 45.7 us  [the longest x1 24.6 us: on_device(): weight = lax.all_to_all(sent, MP, 0, 0).reshape(width, 128)]
    pallas_call x2 -> x3, Pallas kernels: 14.6 us -> 11.4 us  [the longest x1 7.91 us: on_device(): call(functools.partial(score_kernel, dp), [((dp, 16, 128), BF16), ((n_p,...]
where the time goes in v2:
time: 146 us; the launch traced here: 145 us
  blocking collectives  127 us (87%)
  Pallas kernels  12 us (8%)
  local copies, waits for them, and re-layouts  4.88 us (3%)
    all_to_all x1, blocking collectives, on_device(): rx2 = lax.all_to_all(tx2, 'dp', 0, 0)  35.5 us
    all_to_all x1, blocking collectives, on_device(): weight = lax.all_to_all(sent, MP, 0, 0).reshape(width, 128)  24.6 us
    all_to_all x1, blocking collectives, on_device(): rx4 = lax.all_to_all(tx4, 'dp', 0, 0)  21.1 us
    all_to_all x1, blocking collectives, on_device(): terms = lax.all_to_all(gw.reshape(n_mp, rows, 128), MP, 0, 0)  17.6 us
    all_to_all x1, blocking collectives, on_device(): lax.all_to_all(jnp.broadcast_to(mine[None], (dp,) + mine.shape), 'dp', 0, 0)  14.8 us
    all_to_all x1, blocking collectives, on_device(): rx3 = lax.all_to_all(tx3, 'dp', 0, 0)  13.6 us
    pallas_call x1, Pallas kernels, on_device(): call(functools.partial(score_kernel, dp), [((dp, 16, 128), BF16), ((n_p,...  7.91 us
    unnamed x10, local copies, waits for them, and re-layouts  4.15 us

profile of v2, /device:TPU:6, one launch (start us, length us, event | category | flops | bytes accessed | tf_op | source)
XLA Modules:
  0.0 145.5 jit_solution(3834386993342236368)
XLA Ops:
  0.6 0.7 broadcast_in_dim.4
  1.4 24.6 %all_to_all.30 = bf16[64,16,128]{2,1,0:T(8,128)(2,1)S(1)} all-to-all(bf16[64,16,128]{2,1,0:T(8,128)(2,1)S(1)} %broadcast_in_dim.4), channel_id=1, replica_groups=mesh['dp'=12,'x'=4,'y'=8,'core'=2] {'x','y','core'}, dimensions={0} | all-to-all | bytes 524288 | tf_op jit(solution)/shard_map/all_to_all | solution.py:205
  26.0 0.0 copy-start.2
  26.0 0.9 copy-done.2
  26.9 0.0 copy-start.3
  26.9 0.7 copy-done.3
  27.6 0.0 copy-start.4
  27.6 0.7 copy-done.4
  28.3 0.6 shard_map.68
  28.9 35.5 %all_to_all.31.rx_ref.rx2_ref = bf16[12,144,128]{2,1,0:T(8,128)(2,1)S(1)} all-to-all(bf16[12,144,128]{2,1,0:T(8,128)(2,1)S(1)} %get-tuple-element.15), channel_id=1, replica_groups=mesh['dp'=12,'x'=4,'y'=8,'core'=2] {'dp'}, dimensions={0} | all-to-all | bytes 884736 | tf_op jit(solution)/shard_map/all_to_all | solution.py:218
  64.4 0.0 copy-start
  64.4 1.8 %copy-done = bf16[1440,1024]{1,0:T(8,128)(2,1)S(1)} copy-done((bf16[1440,1024]{1,0:T(8,128)(2,1)S(1)}, bf16[1440,1024]{1,0:T(8,128)(2,1)}, u32[]{:S(2)}) %copy-start) | copy-done | bytes 2949144
  66.2 7.9 %shard_map.69 = (bf16[12,16,128]{2,1,0:T(8,128)(2,1)S(1)}, f32[1440,128]{1,0:T(8,128)S(1)}, bf16[1536,1536]{1,0:T(8,128)(2,1)S(1)}, f32[8,1536]{1,0:T(8,128)S(1)...) custom-call(bf16[1440,1024]{1,0:T(8,128)(2,1)S(1)} %copy-done, ...), custom_call_target="tpu_custom_call" | custom-call | tf_op jit(solution)/shard_map/pallas_call | solution.py:219
  74.1 0.0 copy-start.1
  74.1 13.6 %all_to_all.32.rx_ref = bf16[12,16,128]{2,1,0:T(8,128)(2,1)S(1)} all-to-all(bf16[12,16,128]{2,1,0:T(8,128)(2,1)S(1)} %get-tuple-element.16), channel_id=1, replica_groups=mesh['dp'=12,'x'=4,'y'=8,'core'=2] {'dp'}, dimensions={0} | all-to-all | bytes 98304 | tf_op jit(solution)/shard_map/all_to_all | solution.py:241
  87.7 2.4 %shard_map.70 = (bf16[12,128,128]{2,1,0:T(8,128)(2,1)S(1)}, bf16[1440,128]{1,0:T(8,128)(2,1)S(1)}) custom-call(bf16[12,144,128]{2,1,0:T(8,128)(2,1)S(1)} %all_to_all.31.rx_ref.rx2_ref, bf16[12,16,128]{2,1,0:T(8,128)(2,1)S(1)} %all_to_all.32.rx_ref, f32[1440,128]{1,0:T(8,128)S(1)} %get-tuple-element.17.v_ref, ...), custom_call_target="tpu_custom_call" | custom-call | tf_op jit(solution)/shard_map/pallas_call | solution.py:242
  90.2 21.1 %all_to_all.33.rx_ref = bf16[12,128,128]{2,1,0:T(8,128)(2,1)S(1)} all-to-all(bf16[12,128,128]{2,1,0:T(8,128)(2,1)S(1)} %get-tuple-element.23), channel_id=1, replica_groups=mesh['dp'=12,'x'=4,'y'=8,'core'=2] {'dp'}, dimensions={0} | all-to-all | bytes 786432 | tf_op jit(solution)/shard_map/all_to_all | solution.py:248
  111.3 0.0 copy-done.1
  111.3 1.1 shard_map.71
  112.4 17.6 %all_to_all.34 = bf16[64,16,128]{2,1,0:T(8,128)(2,1)S(1)} all-to-all(bf16[64,16,128]{2,1,0:T(8,128)(2,1)S(1)} %bitcast.5), channel_id=1, replica_groups=mesh['dp'=12,'x'=4,'y'=8,'core'=2] {'x','y','core'}, dimensions={0} | all-to-all | bytes 524288 | tf_op jit(solution)/shard_map/all_to_all | solution.py:252
  130.0 0.1 convert_reduce_fusion
  130.1 14.8 %all_to_all.35 = f32[12,16,128]{2,1,0:T(8,128)S(1)} all-to-all(f32[12,16,128]{2,1,0:T(8,128)S(1)} %broadcast_in_dim.5), channel_id=1, replica_groups=mesh['dp'=12,'x'=4,'y'=8,'core'=2] {'dp'}, dimensions={0} | all-to-all | bytes 196608 | tf_op jit(solution)/shard_map/all_to_all | solution.py:254
  144.9 0.6 reduce_sum.19
  (1 shorter events, 0.0 us)
Async XLA Ops:
  26.0 1.0 copy-start.2
  26.9 0.7 copy-start.3
  27.6 0.7 copy-start.4
  64.4 1.8 %copy-start = (bf16[1440,1024]{1,0:T(8,128)(2,1)S(1)}, bf16[1440,1024]{1,0:T(8,128)(2,1)}, u32[]{:S(2)}) copy-start(bf16[1440,1024]{1,0:T(8,128)(2,1)} %hp_ref.1) | copy-start | bytes 8847364
  74.1 37.2 %copy-start.1 = (bf16[1440,1024]{1,0:T(8,128)(2,1)S(1)}, bf16[1440,1024]{1,0:T(8,128)(2,1)}, u32[]{:S(2)}) copy-start(bf16[1440,1024]{1,0:T(8,128)(2,1)} %hp_ref.1) | copy-start | bytes 8847364

commit v3 on v2

--- a/solution.py
+++ b/solution.py
@@ -39,16 +39,13 @@
     return x
 
 
-def query_kernel(dp, n_mp, hq_hbm, w_ref, neg_hbm, rank_hbm, tx_ref, vt_ref, hq, neg_ref, rank_ref, sems):
+def copies_kernel(w_ref, out_ref):
+    for i in range(out_ref.shape[0]):
+        out_ref[i] = w_ref[...]
+
+
+def query_kernel(dp, n_mp, hq_ref, w_ref, neg_ref, rank_ref, tx_ref, vt_ref):
     held = 8
-    copies = [
-        pltpu.make_async_copy(src, dst, sems.at[i])
-        for i, (src, dst) in enumerate(((neg_hbm, neg_ref), (rank_hbm, rank_ref), (hq_hbm, hq)))
-    ]
-    for copy in copies:
-        copy.start()
-    copies[0].wait()
-    copies[1].wait()
     neg = neg_ref[...]
     place = lax.div(neg, held * n_mp) * held + lax.rem(neg, held)
     teach = jnp.exp(-rank_ref[...].astype(F32) / RANK_TEMP)
@@ -66,8 +63,7 @@
     for d in range(dp):
         cut = slice(held * d, held * d + held)
         tx_ref[d, 128:144, :] = jnp.concatenate([high[cut], low[cut]], axis=0).astype(BF16)
-    copies[2].wait()
-    vt = jnp.dot(hq[...], w_ref[...], preferred_element_type=F32).T
+    vt = jnp.dot(hq_ref[...], w_ref[...], preferred_element_type=F32).T
     vt_ref[...] = vt
     et = vt * lax.rsqrt(jnp.sum(vt * vt, axis=0, keepdims=True) + EPS)
     etb = et.astype(BF16)
@@ -75,39 +71,24 @@
         tx_ref[d, 0:128, :] = etb
 
 
-def score_kernel(
-    dp, hp_hbm, w_ref, rx_ref, tx_ref, v_ref, expo_ref, sa_ref, sb_ref, a_ref, b_ref, hp, ef, eb, lhs, sums, sems
-):
+def score_kernel(dp, hp_ref, w_ref, rx_ref, tx_ref, v_ref, expo_ref, sa_ref, sb_ref, a_ref, b_ref, ef, eb, lhs, sums):
     held = 8
-    parts = 3
-    chunk = held * PLEN // parts
-    copies = [
-        pltpu.make_async_copy(
-            hp_hbm.at[pl.ds(chunk * i, chunk)], hp.at[pl.ds(chunk * i, chunk)], sems.at[i]
-        )
-        for i in range(parts)
-    ]
-    for copy in copies:
-        copy.start()
+    v_ref[...] = jnp.dot(hp_ref[...], w_ref[...], preferred_element_type=F32)
     row = lax.broadcasted_iota(jnp.int32, (16, PROWS), 0)
     col = lanes((16, PROWS))
     for p in range(held):
         lhs[p, 128:144, :] = jnp.where((row == p) & (col < PLEN), 1.0, 0.0).astype(BF16)
         ef[p, 176:256, :] = jnp.zeros((80, 128), F32)
     sums[...] = jnp.zeros((16, 128), F32)
-    for i in range(parts):
-        cut = slice(chunk * i, chunk * (i + 1))
-        copies[i].wait()
-        v_ref[cut, :] = jnp.dot(hp[cut, :], w_ref[...], preferred_element_type=F32)
     for p in range(held):
         v = v_ref[PLEN * p : PLEN * (p + 1), :]
         ef[p, 0:PLEN, :] = v * lax.rsqrt(jnp.sum(v * v, axis=1, keepdims=True) + EPS)
         padded = ef[p]
         eb[PROWS * p : PROWS * (p + 1), :] = padded[0:PROWS].astype(BF16)
         lhs[p, 0:128, :] = padded.T[:, 0:PROWS].astype(BF16)
-    for j in range(dp // 2):
-        pair = (2 * j, 2 * j + 1)
-        wide = slice(256 * j, 256 * (j + 1))
+    for j in range(dp // 4):
+        pair = (4 * j, 4 * j + 1, 4 * j + 2, 4 * j + 3)
+        wide = slice(512 * j, 512 * (j + 1))
         q = jnp.concatenate([rx_ref[k, 0:128, :] for k in pair], axis=1)
         codes = jnp.concatenate([rx_ref[k, 128:144, :].astype(F32) for k in pair], axis=1)
         teach = codes[0:8] + codes[8:16]
@@ -185,13 +166,12 @@
     gw_ref[...] = gwt.T.astype(BF16)
 
 
-def call(kernel, outs, scratch=(), far=(), n_in=0, mib=20):
-    specs = [pl.BlockSpec(memory_space=pltpu.HBM if i in far else pltpu.VMEM) for i in range(n_in)]
+def call(kernel, outs, scratch=(), mib=20, gflop=0):
     return pl.pallas_call(
         kernel,
         out_shape=[jax.ShapeDtypeStruct(s, t) for s, t in outs],
-        in_specs=specs,
         scratch_shapes=[pltpu.VMEM(*s) if isinstance(s, tuple) else s for s in scratch],
+        cost_estimate=pl.CostEstimate(flops=gflop * 10**9, bytes_accessed=4 * 10**6, transcendentals=0),
         compiler_params=pltpu.CompilerParams(vmem_limit_bytes=mib * 1024 * 1024),
     )
 
@@ -201,19 +181,10 @@
     width = n_mp * rows
     n_q = dp * 128
     n_p = 8 * PLEN
-    sent = jnp.broadcast_to(proj_weight[None], (n_mp,) + proj_weight.shape)
+    (sent,) = call(copies_kernel, [((n_mp,) + proj_weight.shape, BF16)], gflop=8)(proj_weight)
     weight = lax.all_to_all(sent, MP, 0, 0).reshape(width, 128)
     tx2, vt = call(
-        functools.partial(query_kernel, dp, n_mp),
-        [((dp, 144, 128), BF16), ((128, 128), F32)],
-        [
-            (hq.shape, BF16),
-            (negatives.shape, jnp.int32),
-            (ranks.shape, jnp.int32),
-            pltpu.SemaphoreType.DMA((3,)),
-        ],
-        far=(0, 2, 3),
-        n_in=4,
+        functools.partial(query_kernel, dp, n_mp), [((dp, 144, 128), BF16), ((128, 128), F32)], gflop=4
     )(hq, weight, negatives, ranks)
     rx2 = lax.all_to_all(tx2, "dp", 0, 0)
     tx3, v, expo, sa, sb, a, b = call(
@@ -227,27 +198,19 @@
             ((128, n_q), F32),
             ((128, n_q), F32),
         ],
-        [
-            (hp.shape, BF16),
-            ((8, 256, 128), F32),
-            ((8 * PROWS, 128), BF16),
-            ((8, 144, PROWS), BF16),
-            ((16, 128), F32),
-            pltpu.SemaphoreType.DMA((3,)),
-        ],
-        far=(0,),
-        n_in=3,
+        [((8, 256, 128), F32), ((8 * PROWS, 128), BF16), ((8, 144, PROWS), BF16), ((16, 128), F32)],
+        gflop=2,
     )(hp, weight, rx2)
     rx3 = lax.all_to_all(tx3, "dp", 0, 0)
     tx4, dvp = call(
         functools.partial(passage_kernel, dp),
         [((dp, 128, 128), BF16), ((n_p, 128), BF16)],
         [((n_p, 128), F32)],
-        n_in=8,
+        gflop=1,
     )(rx2, rx3, v, expo, sa, sb, a, b)
     rx4 = lax.all_to_all(tx4, "dp", 0, 0)
     grad_queries, gw = call(
-        functools.partial(grad_kernel, dp), [((128, width), BF16), ((width, 128), BF16)], n_in=6
+        functools.partial(grad_kernel, dp), [((128, width), BF16), ((width, 128), BF16)], gflop=1
     )(hq, hp, weight, rx4, vt, dvp)
     terms = lax.all_to_all(gw.reshape(n_mp, rows, 128), MP, 0, 0)
     mine = jnp.sum(terms.astype(F32), axis=0)

time: 146 us -> 140 us (0.959)
  local copies, waits for them, and re-layouts: 4.88 us -> 0.75 us
  Pallas kernels: 12 us -> 10.5 us
    unnamed x10, local copies, waits for them, and re-layouts: 4.15 us -> 0.74 us
where the time goes in v3:
time: 140 us
  blocking collectives  127 us (91%)
  Pallas kernels  10.5 us (8%)
    all_to_all x1, blocking collectives, on_device(): rx2 = lax.all_to_all(tx2, 'dp', 0, 0)  35.6 us
    all_to_all x1, blocking collectives, on_device(): weight = lax.all_to_all(sent, MP, 0, 0).reshape(width, 128)  24.6 us
    all_to_all x1, blocking collectives, on_device(): rx4 = lax.all_to_all(tx4, 'dp', 0, 0)  21.1 us
    all_to_all x1, blocking collectives, on_device(): terms = lax.all_to_all(gw.reshape(n_mp, rows, 128), MP, 0, 0)  17.7 us
    all_to_all x1, blocking collectives, on_device(): lax.all_to_all(jnp.broadcast_to(mine[None], (dp,) + mine.shape), 'dp', 0, 0)  14.7 us
    all_to_all x1, blocking collectives, on_device(): rx3 = lax.all_to_all(tx3, 'dp', 0, 0)  13.3 us
    pallas_call x1, Pallas kernels, on_device(): call(functools.partial(score_kernel, dp), [((dp, 16, 128), BF16), ((n_p,...  6.58 us

profile of v3, /device:TPU:6, one launch (start us, length us, event | category | flops | bytes accessed | tf_op | source)
XLA Modules:
  0.0 139.6 jit_solution(7731520317759751736)
XLA Ops:
  0.6 0.0 copy-start.1
  0.6 0.0 copy-start.2
  0.7 0.7 copy-done.2
  1.4 0.0 copy-start.3
  1.4 0.0 copy-start.4
  1.4 24.6 %all_to_all.30 = bf16[64,16,128]{2,1,0:T(8,128)(2,1)S(1)} all-to-all(bf16[64,16,128]{2,1,0:T(8,128)(2,1)S(1)} %shard_map.68), channel_id=1, replica_groups=mesh['dp'=12,'x'=4,'y'=8,'core'=2] {'x','y','core'}, dimensions={0} | all-to-all | bytes 524288 | tf_op jit(solution)/shard_map/all_to_all | solution.py:185
  26.0 0.0 copy-done.1
  26.0 0.0 copy-done.3
  26.0 0.0 copy-done.4
  26.0 0.0 copy-start
  26.0 0.3 shard_map.69
  26.4 35.6 %all_to_all.31.rx_ref.rx2_ref = bf16[12,144,128]{2,1,0:T(8,128)(2,1)S(1)} all-to-all(bf16[12,144,128]{2,1,0:T(8,128)(2,1)S(1)} %get-tuple-element.15), channel_id=1, replica_groups=mesh['dp'=12,'x'=4,'y'=8,'core'=2] {'dp'}, dimensions={0} | all-to-all | bytes 884736 | tf_op jit(solution)/shard_map/all_to_all | solution.py:189
  62.0 0.0 copy-done
  62.0 6.6 %shard_map.70 = (bf16[12,16,128]{2,1,0:T(8,128)(2,1)S(1)}, f32[1440,128]{1,0:T(8,128)S(1)}, bf16[1536,1536]{1,0:T(8,128)(2,1)S(1)}, f32[8,1536]{1,0:T(8,128)S(1)...) custom-call(bf16[1440,1024]{1,0:T(8,128)(2,1)S(1)} %copy-done, ...), custom_call_target="tpu_custom_call" | custom-call | flops 2000000000 | bytes 4000000 | tf_op jit(solution)/shard_map/pallas_call | solution.py:190
  68.6 13.3 %all_to_all.32.rx_ref = bf16[12,16,128]{2,1,0:T(8,128)(2,1)S(1)} all-to-all(bf16[12,16,128]{2,1,0:T(8,128)(2,1)S(1)} %get-tuple-element.16), channel_id=1, replica_groups=mesh['dp'=12,'x'=4,'y'=8,'core'=2] {'dp'}, dimensions={0} | all-to-all | bytes 98304 | tf_op jit(solution)/shard_map/all_to_all | solution.py:204
  81.9 2.4 %shard_map.71 = (bf16[12,128,128]{2,1,0:T(8,128)(2,1)S(1)}, bf16[1440,128]{1,0:T(8,128)(2,1)S(1)}) custom-call(bf16[12,144,128]{2,1,0:T(8,128)(2,1)S(1)} %all_to_all.31.rx_ref.rx2_ref, bf16[12,16,128]{2,1,0:T(8,128)(2,1)S(1)} %all_to_all.32.rx_ref, f32[1440,128]{1,0:T(8,128)S(1)} %get-tuple-element.17.v_ref, ...), custom_call_target="tpu_custom_call" | custom-call | flops 1000000000 | bytes 4000000 | tf_op jit(solution)/shard_map/pallas_call | solution.py:205
  84.3 21.1 %all_to_all.33.rx_ref = bf16[12,128,128]{2,1,0:T(8,128)(2,1)S(1)} all-to-all(bf16[12,128,128]{2,1,0:T(8,128)(2,1)S(1)} %get-tuple-element.23), channel_id=1, replica_groups=mesh['dp'=12,'x'=4,'y'=8,'core'=2] {'dp'}, dimensions={0} | all-to-all | bytes 786432 | tf_op jit(solution)/shard_map/all_to_all | solution.py:211
  105.5 1.1 shard_map.72
  106.5 17.7 %all_to_all.34 = bf16[64,16,128]{2,1,0:T(8,128)(2,1)S(1)} all-to-all(bf16[64,16,128]{2,1,0:T(8,128)(2,1)S(1)} %bitcast.5), channel_id=1, replica_groups=mesh['dp'=12,'x'=4,'y'=8,'core'=2] {'x','y','core'}, dimensions={0} | all-to-all | bytes 524288 | tf_op jit(solution)/shard_map/all_to_all | solution.py:215
  124.2 0.1 convert_reduce_fusion
  124.3 14.7 %all_to_all.35 = f32[12,16,128]{2,1,0:T(8,128)S(1)} all-to-all(f32[12,16,128]{2,1,0:T(8,128)S(1)} %broadcast_in_dim.2), channel_id=1, replica_groups=mesh['dp'=12,'x'=4,'y'=8,'core'=2] {'dp'}, dimensions={0} | all-to-all | bytes 196608 | tf_op jit(solution)/shard_map/all_to_all | solution.py:217
  139.0 0.6 reduce_sum.19
  (2 shorter events, 0.0 us)
Async XLA Ops:
  0.6 25.4 %copy-start.1 = (bf16[128,1024]{1,0:T(8,128)(2,1)S(1)}, bf16[128,1024]{1,0:T(8,128)(2,1)}, u32[]{:S(2)}) copy-start(bf16[128,1024]{1,0:T(8,128)(2,1)} %hq_ref.3) | copy-start | bytes 786436
  0.6 0.7 copy-start.2
  1.4 24.7 %copy-start.3 = (s32[4,32]{1,0:T(4,128)S(1)}, s32[4,32]{1,0:T(4,128)}, u32[]{:S(2)}) copy-start(s32[4,32]{1,0:T(4,128)} %neg_ref.1) | copy-start | bytes 1540
  1.4 24.7 %copy-start.4 = (s32[4,32]{1,0:T(4,128)S(1)}, s32[4,32]{1,0:T(4,128)}, u32[]{:S(2)}) copy-start(s32[4,32]{1,0:T(4,128)} %rank_ref.1) | copy-start | bytes 1540
  26.0 36.0 %copy-start = (bf16[1440,1024]{1,0:T(8,128)(2,1)S(1)}, bf16[1440,1024]{1,0:T(8,128)(2,1)}, u32[]{:S(2)}) copy-start(bf16[1440,1024]{1,0:T(8,128)(2,1)} %hp_ref.3) | copy-start | bytes 8847364

commit v4 on v3

--- a/solution.py
+++ b/solution.py
@@ -71,53 +71,36 @@
         tx_ref[d, 0:128, :] = etb
 
 
-def score_kernel(dp, hp_ref, w_ref, rx_ref, tx_ref, v_ref, expo_ref, sa_ref, sb_ref, a_ref, b_ref, ef, eb, lhs, sums):
+def score_kernel(dp, hp_ref, w_ref, rx_ref, tx_ref, v_ref, eb_ref, expo_ref, sa_ref, sb_ref, ef, sums):
     held = 8
     v_ref[...] = jnp.dot(hp_ref[...], w_ref[...], preferred_element_type=F32)
-    row = lax.broadcasted_iota(jnp.int32, (16, PROWS), 0)
-    col = lanes((16, PROWS))
-    for p in range(held):
-        lhs[p, 128:144, :] = jnp.where((row == p) & (col < PLEN), 1.0, 0.0).astype(BF16)
-        ef[p, 176:256, :] = jnp.zeros((80, 128), F32)
+    for p in range(held):
+        v = v_ref[PLEN * p : PLEN * (p + 1), :]
+        ef[PROWS * (p + 1) - 16 : PROWS * (p + 1), :] = jnp.zeros((16, 128), F32)
+        ef[PROWS * p : PROWS * p + PLEN, :] = v * lax.rsqrt(jnp.sum(v * v, axis=1, keepdims=True) + EPS)
+    eb_ref[...] = ef[...].astype(BF16)
+    q = jnp.concatenate([rx_ref[k, 0:128, :] for k in range(dp)], axis=1)
+    codes = jnp.concatenate([rx_ref[k, 128:144, :].astype(F32) for k in range(dp)], axis=1)
+    teach = codes[0:8] + codes[8:16]
+    dots = jnp.dot(eb_ref[...], q, preferred_element_type=F32)
+    row = lax.broadcasted_iota(jnp.int32, (8, 128 * dp), 0)
+    total = jnp.zeros((8, 128 * dp), F32)
+    for p in range(held):
+        cut = slice(PROWS * p, PROWS * (p + 1))
+        expo = jnp.exp2(dots[cut] * (LOG2E / TAU))
+        expo_ref[cut, :] = expo.astype(BF16)
+        part = jnp.where(row < PLEN - 176, expo[176:184], 0.0)
+        for i in range(22):
+            part = part + expo[8 * i : 8 * (i + 1)]
+        total = jnp.where(row == p, jnp.sum(part, axis=0, keepdims=True), total)
+    score = query_sums(TAU * jnp.log(total))
+    es = jnp.where(teach > 0.0, jnp.exp(score), 0.0)
+    sa_ref[...] = es / total
+    sb_ref[...] = teach / total
+    listed = jnp.sum(es, axis=0, keepdims=True)
     sums[...] = jnp.zeros((16, 128), F32)
-    for p in range(held):
-        v = v_ref[PLEN * p : PLEN * (p + 1), :]
-        ef[p, 0:PLEN, :] = v * lax.rsqrt(jnp.sum(v * v, axis=1, keepdims=True) + EPS)
-        padded = ef[p]
-        eb[PROWS * p : PROWS * (p + 1), :] = padded[0:PROWS].astype(BF16)
-        lhs[p, 0:128, :] = padded.T[:, 0:PROWS].astype(BF16)
-    for j in range(dp // 4):
-        pair = (4 * j, 4 * j + 1, 4 * j + 2, 4 * j + 3)
-        wide = slice(512 * j, 512 * (j + 1))
-        q = jnp.concatenate([rx_ref[k, 0:128, :] for k in pair], axis=1)
-        codes = jnp.concatenate([rx_ref[k, 128:144, :].astype(F32) for k in pair], axis=1)
-        teach = codes[0:8] + codes[8:16]
-        listed = teach > 0.0
-        dots = jnp.dot(eb[...], q, preferred_element_type=F32)
-        expo = jnp.exp2(dots * (LOG2E / TAU)).astype(BF16)
-        expo_ref[:, wide] = expo
-        near = []
-        total = None
-        for p in range(held):
-            out = jnp.dot(lhs[p], expo[PROWS * p : PROWS * (p + 1)], preferred_element_type=F32)
-            near.append(out[0:128])
-            total = out[128:136] if p == 0 else total + out[128:136]
-        score = query_sums(TAU * jnp.log(total))
-        es = jnp.where(listed, jnp.exp(score), 0.0)
-        sa = es / total
-        sb = teach / total
-        sa_ref[:, wide] = sa
-        sb_ref[:, wide] = sb
-        a = near[0] * sa[0:1]
-        b = near[0] * sb[0:1]
-        for p in range(1, held):
-            a = a + near[p] * sa[p : p + 1]
-            b = b + near[p] * sb[p : p + 1]
-        a_ref[:, wide] = a
-        b_ref[:, wide] = b
-        part = jnp.sum(es, axis=0, keepdims=True)
-        for h, k in enumerate(pair):
-            sums[k : k + 1, :] = part[:, 128 * h : 128 * (h + 1)]
+    for k in range(dp):
+        sums[k : k + 1, :] = listed[:, 128 * k : 128 * (k + 1)]
     whole = sums[...]
     high = whole.astype(BF16).astype(F32)
     rest = whole - high
@@ -129,22 +112,24 @@
         tx_ref[d] = coded.astype(BF16)
 
 
-def passage_kernel(dp, rx2_ref, rx_ref, v_ref, expo_ref, sa_ref, sb_ref, a_ref, b_ref, tx_ref, dv_ref, dv):
+def passage_kernel(dp, rx2_ref, rx_ref, v_ref, eb_ref, expo_ref, sa_ref, sb_ref, tx_ref, dv_ref, mixed, dv):
     held = 8
     part = rx_ref[0].astype(F32)
     for s in range(1, dp):
         part = part + rx_ref[s].astype(F32)
     sums = query_sums(part)
     inv = 1.0 / jnp.where(sums > 0.0, sums, 1.0)
-    for k in range(dp):
-        cut = slice(128 * k, 128 * (k + 1))
-        tx_ref[k] = (a_ref[:, cut] * inv[k : k + 1] - b_ref[:, cut]).astype(BF16)
-    qt = jnp.concatenate([rx2_ref[k, 0:128, :] for k in range(dp)], axis=1).astype(F32)
     wide_inv = jnp.concatenate([inv[k : k + 1] for k in range(dp)], axis=1)
     share = sa_ref[...] * wide_inv - sb_ref[...]
     for p in range(held):
-        scaled = (qt * share[p : p + 1]).astype(BF16)
-        dep = contract(expo_ref[PROWS * p : PROWS * (p + 1), :], scaled, ((1,), (1,)))[0:PLEN]
+        cut = slice(PROWS * p, PROWS * (p + 1))
+        mixed[cut, :] = (expo_ref[cut, :].astype(F32) * share[p : p + 1]).astype(BF16)
+    deq = contract(eb_ref[...], mixed[...], ((0,), (0,))).astype(BF16)
+    for k in range(dp):
+        tx_ref[k] = deq[:, 128 * k : 128 * (k + 1)]
+    qt = jnp.concatenate([rx2_ref[k, 0:128, :] for k in range(dp)], axis=1)
+    for p in range(held):
+        dep = contract(mixed[PROWS * p : PROWS * (p + 1), :], qt, ((1,), (1,)))[0:PLEN]
         v = v_ref[PLEN * p : PLEN * (p + 1), :]
         rp = lax.rsqrt(jnp.sum(v * v, axis=1, keepdims=True) + EPS)
         e = v * rp
@@ -166,6 +151,21 @@
     gw_ref[...] = gwt.T.astype(BF16)
 
 
+def share_kernel(terms_ref, tx_ref):
+    mine = terms_ref[0].astype(F32)
+    for m in range(1, terms_ref.shape[0]):
+        mine = mine + terms_ref[m].astype(F32)
+    for d in range(tx_ref.shape[0]):
+        tx_ref[d] = mine
+
+
+def sum_kernel(shares_ref, out_ref):
+    total = shares_ref[0]
+    for d in range(1, shares_ref.shape[0]):
+        total = total + shares_ref[d]
+    out_ref[...] = total
+
+
 def call(kernel, outs, scratch=(), mib=20, gflop=0):
     return pl.pallas_call(
         kernel,
@@ -187,35 +187,36 @@
         functools.partial(query_kernel, dp, n_mp), [((dp, 144, 128), BF16), ((128, 128), F32)], gflop=4
     )(hq, weight, negatives, ranks)
     rx2 = lax.all_to_all(tx2, "dp", 0, 0)
-    tx3, v, expo, sa, sb, a, b = call(
+    tx3, v, eb, expo, sa, sb = call(
         functools.partial(score_kernel, dp),
         [
             ((dp, 16, 128), BF16),
             ((n_p, 128), F32),
+            ((8 * PROWS, 128), BF16),
             ((8 * PROWS, n_q), BF16),
             ((8, n_q), F32),
             ((8, n_q), F32),
-            ((128, n_q), F32),
-            ((128, n_q), F32),
         ],
-        [((8, 256, 128), F32), ((8 * PROWS, 128), BF16), ((8, 144, PROWS), BF16), ((16, 128), F32)],
+        [((8 * PROWS, 128), F32), ((16, 128), F32)],
+        mib=28,
         gflop=2,
     )(hp, weight, rx2)
     rx3 = lax.all_to_all(tx3, "dp", 0, 0)
     tx4, dvp = call(
         functools.partial(passage_kernel, dp),
         [((dp, 128, 128), BF16), ((n_p, 128), BF16)],
-        [((n_p, 128), F32)],
+        [((8 * PROWS, n_q), BF16), ((n_p, 128), F32)],
         gflop=1,
-    )(rx2, rx3, v, expo, sa, sb, a, b)
+    )(rx2, rx3, v, eb, expo, sa, sb)
     rx4 = lax.all_to_all(tx4, "dp", 0, 0)
     grad_queries, gw = call(
         functools.partial(grad_kernel, dp), [((128, width), BF16), ((width, 128), BF16)], gflop=1
     )(hq, hp, weight, rx4, vt, dvp)
     terms = lax.all_to_all(gw.reshape(n_mp, rows, 128), MP, 0, 0)
-    mine = jnp.sum(terms.astype(F32), axis=0)
-    shares = lax.all_to_all(jnp.broadcast_to(mine[None], (dp,) + mine.shape), "dp", 0, 0)
-    return grad_queries, jnp.sum(shares, axis=0)
+    (tx5,) = call(share_kernel, [((dp, rows, 128), F32)])(terms)
+    shares = lax.all_to_all(tx5, "dp", 0, 0)
+    (grad_weight,) = call(sum_kernel, [((rows, 128), F32)])(shares)
+    return grad_queries, grad_weight
 
 
 def solution(mesh):

time: 140 us -> 139 us (level)
    pallas_call x1, Pallas kernels: 6.58 us -> 4.45 us  [on_device(): call(functools.partial(score_kernel, dp), [((dp, 16, 128), BF16), ((n_p,...]
where the time goes in v4:
time: 139 us; the launch traced here: 138 us
  blocking collectives  127 us (91%)
  Pallas kernels  9.87 us (7%)
    all_to_all x1, blocking collectives, on_device(): rx2 = lax.all_to_all(tx2, 'dp', 0, 0)  35.6 us
    all_to_all x1, blocking collectives, on_device(): weight = lax.all_to_all(sent, MP, 0, 0).reshape(width, 128)  24.6 us
    all_to_all x1, blocking collectives, on_device(): rx4 = lax.all_to_all(tx4, 'dp', 0, 0)  21.1 us
    all_to_all x1, blocking collectives, on_device(): terms = lax.all_to_all(gw.reshape(n_mp, rows, 128), MP, 0, 0)  17.6 us
    all_to_all x1, blocking collectives, on_device(): shares = lax.all_to_all(tx5, 'dp', 0, 0)  14.8 us
    all_to_all x1, blocking collectives, on_device(): rx3 = lax.all_to_all(tx3, 'dp', 0, 0)  13.3 us
    pallas_call x1, Pallas kernels, on_device(): call(functools.partial(score_kernel, dp), [((dp, 16, 128), BF16), ((n_p,...  4.45 us
    pallas_call x1, Pallas kernels, on_device(): call(functools.partial(passage_kernel, dp), [((dp, 128, 128), BF16), ((n_...  3.28 us

profile of v4, /device:TPU:6, one launch (start us, length us, event | category | flops | bytes accessed | tf_op | source)
XLA Modules:
  0.0 138.4 jit_solution(2886354395998915270)
XLA Ops:
  0.6 0.0 copy-start.1
  0.6 0.0 copy-start.2
  0.7 0.7 copy-done.2
  1.4 0.0 copy-start.3
  1.4 0.0 copy-start.4
  1.4 24.6 %all_to_all.30 = bf16[64,16,128]{2,1,0:T(8,128)(2,1)S(1)} all-to-all(bf16[64,16,128]{2,1,0:T(8,128)(2,1)S(1)} %shard_map.68), channel_id=1, replica_groups=mesh['dp'=12,'x'=4,'y'=8,'core'=2] {'x','y','core'}, dimensions={0} | all-to-all | bytes 524288 | tf_op jit(solution)/shard_map/all_to_all | solution.py:185
  26.0 0.0 copy-done.1
  26.0 0.0 copy-done.3
  26.0 0.0 copy-done.4
  26.0 0.0 copy-start
  26.0 0.3 shard_map.69
  26.4 35.6 %all_to_all.31.rx_ref.rx2_ref = bf16[12,144,128]{2,1,0:T(8,128)(2,1)S(1)} all-to-all(bf16[12,144,128]{2,1,0:T(8,128)(2,1)S(1)} %get-tuple-element.14), channel_id=1, replica_groups=mesh['dp'=12,'x'=4,'y'=8,'core'=2] {'dp'}, dimensions={0} | all-to-all | bytes 884736 | tf_op jit(solution)/shard_map/all_to_all | solution.py:189
  62.0 0.0 copy-done
  62.0 4.4 %shard_map.70 = (bf16[12,16,128]{2,1,0:T(8,128)(2,1)S(1)}, f32[1440,128]{1,0:T(8,128)S(1)}, bf16[1536,128]{1,0:T(8,128)(2,1)S(1)}, bf16[1536,1536]{1,0:T(8,128)(...) custom-call(bf16[1440,1024]{1,0:T(8,128)(2,1)S(1)} %copy-done, bf16[1024,128]{1,0:T(8,128)(2,1)S(1)} %bitcast.3, ...), custom_call_target="tpu_custom_call" | custom-call | flops 2000000000 | bytes 4000000 | tf_op jit(solution)/shard_map/pallas_call | solution.py:190
  66.5 13.3 %all_to_all.32.rx_ref = bf16[12,16,128]{2,1,0:T(8,128)(2,1)S(1)} all-to-all(bf16[12,16,128]{2,1,0:T(8,128)(2,1)S(1)} %get-tuple-element.15), channel_id=1, replica_groups=mesh['dp'=12,'x'=4,'y'=8,'core'=2] {'dp'}, dimensions={0} | all-to-all | bytes 98304 | tf_op jit(solution)/shard_map/all_to_all | solution.py:204
  79.8 3.3 %shard_map.71 = (bf16[12,128,128]{2,1,0:T(8,128)(2,1)S(1)}, bf16[1440,128]{1,0:T(8,128)(2,1)S(1)}) custom-call(bf16[12,144,128]{2,1,0:T(8,128)(2,1)S(1)} %all_to_all.31.rx_ref.rx2_ref, bf16[12,16,128]{2,1,0:T(8,128)(2,1)S(1)} %all_to_all.32.rx_ref, f32[1440,128]{1,0:T(8,128)S(1)} %get-tuple-element.16.v_ref, bf16[1536,128]{1,0:T(8,128)(2,1)S(1)} %get-tuple-element.17.eb_ref, ...), custom_call_target="tpu_custom_call" | custom-call | flops 1000000000 | bytes 4000000 | tf_op jit(solution)/shard_map/pallas_call | solution.py:205
  83.1 21.1 %all_to_all.33.rx_ref = bf16[12,128,128]{2,1,0:T(8,128)(2,1)S(1)} all-to-all(bf16[12,128,128]{2,1,0:T(8,128)(2,1)S(1)} %get-tuple-element.21), channel_id=1, replica_groups=mesh['dp'=12,'x'=4,'y'=8,'core'=2] {'dp'}, dimensions={0} | all-to-all | bytes 786432 | tf_op jit(solution)/shard_map/all_to_all | solution.py:211
  104.2 1.1 shard_map.72
  105.3 17.6 %all_to_all.34.terms_ref = bf16[64,16,128]{2,1,0:T(8,128)(2,1)S(1)} all-to-all(bf16[64,16,128]{2,1,0:T(8,128)(2,1)S(1)} %bitcast.5), channel_id=1, replica_groups=mesh['dp'=12,'x'=4,'y'=8,'core'=2] {'x','y','core'}, dimensions={0} | all-to-all | bytes 524288 | tf_op jit(solution)/shard_map/all_to_all | solution.py:215
  122.9 0.1 shard_map.73
  123.0 14.8 %all_to_all.35.shares_ref = f32[12,16,128]{2,1,0:T(8,128)S(1)} all-to-all(f32[12,16,128]{2,1,0:T(8,128)S(1)} %shard_map.73), channel_id=1, replica_groups=mesh['dp'=12,'x'=4,'y'=8,'core'=2] {'dp'}, dimensions={0} | all-to-all | bytes 196608 | tf_op jit(solution)/shard_map/all_to_all | solution.py:217
  137.7 0.6 shard_map.74
  (1 shorter events, 0.0 us)
Async XLA Ops:
  0.6 25.4 %copy-start.1 = (bf16[128,1024]{1,0:T(8,128)(2,1)S(1)}, bf16[128,1024]{1,0:T(8,128)(2,1)}, u32[]{:S(2)}) copy-start(bf16[128,1024]{1,0:T(8,128)(2,1)} %hq_ref.3) | copy-start | bytes 786436
  0.6 0.7 copy-start.2
  1.4 24.7 %copy-start.3 = (s32[4,32]{1,0:T(4,128)S(1)}, s32[4,32]{1,0:T(4,128)}, u32[]{:S(2)}) copy-start(s32[4,32]{1,0:T(4,128)} %neg_ref.1) | copy-start | bytes 1540
  1.4 24.7 %copy-start.4 = (s32[4,32]{1,0:T(4,128)S(1)}, s32[4,32]{1,0:T(4,128)}, u32[]{:S(2)}) copy-start(s32[4,32]{1,0:T(4,128)} %rank_ref.1) | copy-start | bytes 1540
  26.0 36.0 %copy-start = (bf16[1440,1024]{1,0:T(8,128)(2,1)S(1)}, bf16[1440,1024]{1,0:T(8,128)(2,1)}, u32[]{:S(2)}) copy-start(bf16[1440,1024]{1,0:T(8,128)(2,1)} %hp_ref.3) | copy-start | bytes 8847364

commit v5 on v4

--- a/solution.py
+++ b/solution.py
@@ -59,10 +59,9 @@
         column = jnp.sum(mine, axis=1, keepdims=True)
         table = jnp.where(lane // QLEN == q, column, table)
     high = table.astype(BF16).astype(F32)
-    low = table - high
+    halves = jnp.where(lane % QLEN < QLEN // 2, high, table - high)
     for d in range(dp):
-        cut = slice(held * d, held * d + held)
-        tx_ref[d, 128:144, :] = jnp.concatenate([high[cut], low[cut]], axis=0).astype(BF16)
+        tx_ref[d, 128:136, :] = halves[held * d : held * d + held].astype(BF16)
     vt = jnp.dot(hq_ref[...], w_ref[...], preferred_element_type=F32).T
     vt_ref[...] = vt
     et = vt * lax.rsqrt(jnp.sum(vt * vt, axis=0, keepdims=True) + EPS)
@@ -80,8 +79,12 @@
         ef[PROWS * p : PROWS * p + PLEN, :] = v * lax.rsqrt(jnp.sum(v * v, axis=1, keepdims=True) + EPS)
     eb_ref[...] = ef[...].astype(BF16)
     q = jnp.concatenate([rx_ref[k, 0:128, :] for k in range(dp)], axis=1)
-    codes = jnp.concatenate([rx_ref[k, 128:144, :].astype(F32) for k in range(dp)], axis=1)
-    teach = codes[0:8] + codes[8:16]
+    codes = jnp.concatenate([rx_ref[k, 128:136, :].astype(F32) for k in range(dp)], axis=1)
+    half = QLEN // 2
+    other = jnp.where(
+        lanes(codes.shape) % QLEN < half, pltpu.roll(codes, 128 * dp - half, 1), pltpu.roll(codes, half, 1)
+    )
+    teach = codes + other
     dots = jnp.dot(eb_ref[...], q, preferred_element_type=F32)
     row = lax.broadcasted_iota(jnp.int32, (8, 128 * dp), 0)
     total = jnp.zeros((8, 128 * dp), F32)
@@ -184,7 +187,7 @@
     (sent,) = call(copies_kernel, [((n_mp,) + proj_weight.shape, BF16)], gflop=8)(proj_weight)
     weight = lax.all_to_all(sent, MP, 0, 0).reshape(width, 128)
     tx2, vt = call(
-        functools.partial(query_kernel, dp, n_mp), [((dp, 144, 128), BF16), ((128, 128), F32)], gflop=4
+        functools.partial(query_kernel, dp, n_mp), [((dp, 136, 128), BF16), ((128, 128), F32)], gflop=4
     )(hq, weight, negatives, ranks)
     rx2 = lax.all_to_all(tx2, "dp", 0, 0)
     tx3, v, eb, expo, sa, sb = call(

time: 139 us -> 138 us (level)
  no operation moved by 1% of the time
where the time goes in v5:
time: 138 us
  blocking collectives  126 us (91%)
  Pallas kernels  9.93 us (7%)
    all_to_all x1, blocking collectives, on_device(): rx2 = lax.all_to_all(tx2, 'dp', 0, 0)  34.9 us
    all_to_all x1, blocking collectives, on_device(): weight = lax.all_to_all(sent, MP, 0, 0).reshape(width, 128)  24.6 us
    all_to_all x1, blocking collectives, on_device(): rx4 = lax.all_to_all(tx4, 'dp', 0, 0)  20.9 us
    all_to_all x1, blocking collectives, on_device(): terms = lax.all_to_all(gw.reshape(n_mp, rows, 128), MP, 0, 0)  17.6 us
    all_to_all x1, blocking collectives, on_device(): shares = lax.all_to_all(tx5, 'dp', 0, 0)  14.8 us
    all_to_all x1, blocking collectives, on_device(): rx3 = lax.all_to_all(tx3, 'dp', 0, 0)  13.3 us
    pallas_call x1, Pallas kernels, on_device(): call(functools.partial(score_kernel, dp), [((dp, 16, 128), BF16), ((n_p,...  4.47 us
    pallas_call x1, Pallas kernels, on_device(): call(functools.partial(passage_kernel, dp), [((dp, 128, 128), BF16), ((n_...  3.32 us

profile of v5, /device:TPU:6, one launch (start us, length us, event | category | flops | bytes accessed | tf_op | source)
XLA Modules:
  0.0 137.5 jit_solution(2664880714394959041)
XLA Ops:
  0.6 0.0 copy-start.1
  0.6 0.0 copy-start.2
  0.7 0.7 copy-done.2
  1.4 0.0 copy-start.3
  1.4 0.0 copy-start.4
  1.4 24.6 %all_to_all.30 = bf16[64,16,128]{2,1,0:T(8,128)(2,1)S(1)} all-to-all(bf16[64,16,128]{2,1,0:T(8,128)(2,1)S(1)} %shard_map.68), channel_id=1, replica_groups=mesh['dp'=12,'x'=4,'y'=8,'core'=2] {'x','y','core'}, dimensions={0} | all-to-all | bytes 524288 | tf_op jit(solution)/shard_map/all_to_all | solution.py:188
  26.0 0.0 copy-done.1
  26.0 0.0 copy-done.3
  26.0 0.0 copy-done.4
  26.0 0.0 copy-start
  26.0 0.3 shard_map.69
  26.4 34.9 %all_to_all.31.rx_ref.rx2_ref = bf16[12,136,128]{2,1,0:T(8,128)(2,1)S(1)} all-to-all(bf16[12,136,128]{2,1,0:T(8,128)(2,1)S(1)} %get-tuple-element.14), channel_id=1, replica_groups=mesh['dp'=12,'x'=4,'y'=8,'core'=2] {'dp'}, dimensions={0} | all-to-all | bytes 835584 | tf_op jit(solution)/shard_map/all_to_all | solution.py:192
  61.3 0.0 copy-done
  61.3 4.5 %shard_map.70 = (bf16[12,16,128]{2,1,0:T(8,128)(2,1)S(1)}, f32[1440,128]{1,0:T(8,128)S(1)}, bf16[1536,128]{1,0:T(8,128)(2,1)S(1)}, bf16[1536,1536]{1,0:T(8,128)(...) custom-call(bf16[1440,1024]{1,0:T(8,128)(2,1)S(1)} %copy-done, bf16[1024,128]{1,0:T(8,128)(2,1)S(1)} %bitcast.3, ...), custom_call_target="tpu_custom_call" | custom-call | flops 2000000000 | bytes 4000000 | tf_op jit(solution)/shard_map/pallas_call | solution.py:193
  65.8 13.3 %all_to_all.32.rx_ref = bf16[12,16,128]{2,1,0:T(8,128)(2,1)S(1)} all-to-all(bf16[12,16,128]{2,1,0:T(8,128)(2,1)S(1)} %get-tuple-element.15), channel_id=1, replica_groups=mesh['dp'=12,'x'=4,'y'=8,'core'=2] {'dp'}, dimensions={0} | all-to-all | bytes 98304 | tf_op jit(solution)/shard_map/all_to_all | solution.py:207
  79.1 3.3 %shard_map.71 = (bf16[12,128,128]{2,1,0:T(8,128)(2,1)S(1)}, bf16[1440,128]{1,0:T(8,128)(2,1)S(1)}) custom-call(bf16[12,136,128]{2,1,0:T(8,128)(2,1)S(1)} %all_to_all.31.rx_ref.rx2_ref, bf16[12,16,128]{2,1,0:T(8,128)(2,1)S(1)} %all_to_all.32.rx_ref, f32[1440,128]{1,0:T(8,128)S(1)} %get-tuple-element.16.v_ref, bf16[1536,128]{1,0:T(8,128)(2,1)S(1)} %get-tuple-element.17.eb_ref, ...), custom_call_target="tpu_custom_call" | custom-call | flops 1000000000 | bytes 4000000 | tf_op jit(solution)/shard_map/pallas_call | solution.py:208
  82.4 20.9 %all_to_all.33.rx_ref = bf16[12,128,128]{2,1,0:T(8,128)(2,1)S(1)} all-to-all(bf16[12,128,128]{2,1,0:T(8,128)(2,1)S(1)} %get-tuple-element.21), channel_id=1, replica_groups=mesh['dp'=12,'x'=4,'y'=8,'core'=2] {'dp'}, dimensions={0} | all-to-all | bytes 786432 | tf_op jit(solution)/shard_map/all_to_all | solution.py:214
  103.3 1.1 shard_map.72
  104.4 17.6 %all_to_all.34.terms_ref = bf16[64,16,128]{2,1,0:T(8,128)(2,1)S(1)} all-to-all(bf16[64,16,128]{2,1,0:T(8,128)(2,1)S(1)} %bitcast.5), channel_id=1, replica_groups=mesh['dp'=12,'x'=4,'y'=8,'core'=2] {'x','y','core'}, dimensions={0} | all-to-all | bytes 524288 | tf_op jit(solution)/shard_map/all_to_all | solution.py:218
  122.0 0.1 shard_map.73
  122.1 14.8 %all_to_all.35.shares_ref = f32[12,16,128]{2,1,0:T(8,128)S(1)} all-to-all(f32[12,16,128]{2,1,0:T(8,128)S(1)} %shard_map.73), channel_id=1, replica_groups=mesh['dp'=12,'x'=4,'y'=8,'core'=2] {'dp'}, dimensions={0} | all-to-all | bytes 196608 | tf_op jit(solution)/shard_map/all_to_all | solution.py:220
  136.9 0.6 shard_map.74
  (1 shorter events, 0.0 us)
Async XLA Ops:
  0.6 25.4 %copy-start.1 = (bf16[128,1024]{1,0:T(8,128)(2,1)S(1)}, bf16[128,1024]{1,0:T(8,128)(2,1)}, u32[]{:S(2)}) copy-start(bf16[128,1024]{1,0:T(8,128)(2,1)} %hq_ref.3) | copy-start | bytes 786436
  0.6 0.7 copy-start.2
  1.4 24.7 %copy-start.3 = (s32[4,32]{1,0:T(4,128)S(1)}, s32[4,32]{1,0:T(4,128)}, u32[]{:S(2)}) copy-start(s32[4,32]{1,0:T(4,128)} %neg_ref.1) | copy-start | bytes 1540
  1.4 24.7 %copy-start.4 = (s32[4,32]{1,0:T(4,128)S(1)}, s32[4,32]{1,0:T(4,128)}, u32[]{:S(2)}) copy-start(s32[4,32]{1,0:T(4,128)} %rank_ref.1) | copy-start | bytes 1540
  26.0 35.3 %copy-start = (bf16[1440,1024]{1,0:T(8,128)(2,1)S(1)}, bf16[1440,1024]{1,0:T(8,128)(2,1)}, u32[]{:S(2)}) copy-start(bf16[1440,1024]{1,0:T(8,128)(2,1)} %hp_ref.3) | copy-start | bytes 8847364

commit v6 on v5

--- a/solution.py
+++ b/solution.py
@@ -111,8 +111,9 @@
     low = rest - mid
     at = lanes((16, 128)) % QLEN
     coded = jnp.where(at == 0, high, jnp.where(at == 1, mid, jnp.where(at == 2, low, 0.0)))
+    packed = (coded[0:8] + pltpu.roll(coded[8:16], QLEN // 2, 1)).astype(BF16)
     for d in range(dp):
-        tx_ref[d] = coded.astype(BF16)
+        tx_ref[d] = packed
 
 
 def passage_kernel(dp, rx2_ref, rx_ref, v_ref, eb_ref, expo_ref, sa_ref, sb_ref, tx_ref, dv_ref, mixed, dv):
@@ -120,7 +121,8 @@
     part = rx_ref[0].astype(F32)
     for s in range(1, dp):
         part = part + rx_ref[s].astype(F32)
-    sums = query_sums(part)
+    first = lanes(part.shape) % QLEN < QLEN // 2
+    sums = query_sums(jnp.concatenate([jnp.where(first, part, 0.0), jnp.where(first, 0.0, part)], axis=0))
     inv = 1.0 / jnp.where(sums > 0.0, sums, 1.0)
     wide_inv = jnp.concatenate([inv[k : k + 1] for k in range(dp)], axis=1)
     share = sa_ref[...] * wide_inv - sb_ref[...]
@@ -158,14 +160,15 @@
     mine = terms_ref[0].astype(F32)
     for m in range(1, terms_ref.shape[0]):
         mine = mine + terms_ref[m].astype(F32)
+    sent = mine.astype(BF16)
     for d in range(tx_ref.shape[0]):
-        tx_ref[d] = mine
+        tx_ref[d] = sent
 
 
 def sum_kernel(shares_ref, out_ref):
-    total = shares_ref[0]
+    total = shares_ref[0].astype(F32)
     for d in range(1, shares_ref.shape[0]):
-        total = total + shares_ref[d]
+        total = total + shares_ref[d].astype(F32)
     out_ref[...] = total
 
 
@@ -193,7 +196,7 @@
     tx3, v, eb, expo, sa, sb = call(
         functools.partial(score_kernel, dp),
         [
-            ((dp, 16, 128), BF16),
+            ((dp, 8, 128), BF16),
             ((n_p, 128), F32),
             ((8 * PROWS, 128), BF16),
             ((8 * PROWS, n_q), BF16),
@@ -216,7 +219,7 @@
         functools.partial(grad_kernel, dp), [((128, width), BF16), ((width, 128), BF16)], gflop=1
     )(hq, hp, weight, rx4, vt, dvp)
     terms = lax.all_to_all(gw.reshape(n_mp, rows, 128), MP, 0, 0)
-    (tx5,) = call(share_kernel, [((dp, rows, 128), F32)])(terms)
+    (tx5,) = call(share_kernel, [((dp, rows, 128), BF16)])(terms)
     shares = lax.all_to_all(tx5, "dp", 0, 0)
     (grad_weight,) = call(sum_kernel, [((rows, 128), F32)])(shares)
     return grad_queries, grad_weight

time: 138 us -> 137 us (level)
  no operation moved by 1% of the time
where the time goes in v6:
time: 137 us; the launch traced here: 136 us
  blocking collectives  125 us (91%)
  Pallas kernels  9.95 us (7%)
    all_to_all x1, blocking collectives, on_device(): rx2 = lax.all_to_all(tx2, 'dp', 0, 0)  34.9 us
    all_to_all x1, blocking collectives, on_device(): weight = lax.all_to_all(sent, MP, 0, 0).reshape(width, 128)  24.6 us
    all_to_all x1, blocking collectives, on_device(): rx4 = lax.all_to_all(tx4, 'dp', 0, 0)  20.9 us
    all_to_all x1, blocking collectives, on_device(): terms = lax.all_to_all(gw.reshape(n_mp, rows, 128), MP, 0, 0)  17.6 us
    all_to_all x1, blocking collectives, on_device(): shares = lax.all_to_all(tx5, 'dp', 0, 0)  14 us
    all_to_all x1, blocking collectives, on_device(): rx3 = lax.all_to_all(tx3, 'dp', 0, 0)  12.9 us
    pallas_call x1, Pallas kernels, on_device(): call(functools.partial(score_kernel, dp), [((dp, 8, 128), BF16), ((n_p, 1...  4.52 us
    pallas_call x1, Pallas kernels, on_device(): call(functools.partial(passage_kernel, dp), [((dp, 128, 128), BF16), ((n_...  3.28 us

profile of v6, /device:TPU:6, one launch (start us, length us, event | category | flops | bytes accessed | tf_op | source)
XLA Modules:
  0.0 136.4 jit_solution(5812322655554328832)
XLA Ops:
  0.6 0.0 copy-start.1
  0.6 0.0 copy-start.2
  0.7 0.7 copy-done.2
  1.4 0.0 copy-start.3
  1.4 0.0 copy-start.4
  1.4 24.6 %all_to_all.30 = bf16[64,16,128]{2,1,0:T(8,128)(2,1)S(1)} all-to-all(bf16[64,16,128]{2,1,0:T(8,128)(2,1)S(1)} %shard_map.68), channel_id=1, replica_groups=mesh['dp'=12,'x'=4,'y'=8,'core'=2] {'x','y','core'}, dimensions={0} | all-to-all | bytes 524288 | tf_op jit(solution)/shard_map/all_to_all | solution.py:191
  26.0 0.0 copy-done.1
  26.0 0.0 copy-done.3
  26.0 0.0 copy-done.4
  26.0 0.0 copy-start
  26.0 0.3 shard_map.69
  26.4 34.9 %all_to_all.31.rx_ref.rx2_ref = bf16[12,136,128]{2,1,0:T(8,128)(2,1)S(1)} all-to-all(bf16[12,136,128]{2,1,0:T(8,128)(2,1)S(1)} %get-tuple-element.14), channel_id=1, replica_groups=mesh['dp'=12,'x'=4,'y'=8,'core'=2] {'dp'}, dimensions={0} | all-to-all | bytes 835584 | tf_op jit(solution)/shard_map/all_to_all | solution.py:195
  61.3 0.0 copy-done
  61.3 4.5 %shard_map.70 = (bf16[12,8,128]{2,1,0:T(8,128)(2,1)S(1)}, f32[1440,128]{1,0:T(8,128)S(1)}, bf16[1536,128]{1,0:T(8,128)(2,1)S(1)}, bf16[1536,1536]{1,0:T(8,128)(2...) custom-call(bf16[1440,1024]{1,0:T(8,128)(2,1)S(1)} %copy-done, bf16[1024,128]{1,0:T(8,128)(2,1)S(1)} %bitcast.3, ...), custom_call_target="tpu_custom_call" | custom-call | flops 2000000000 | bytes 4000000 | tf_op jit(solution)/shard_map/pallas_call | solution.py:196
  65.8 12.9 %all_to_all.32.rx_ref = bf16[12,8,128]{2,1,0:T(8,128)(2,1)S(1)} all-to-all(bf16[12,8,128]{2,1,0:T(8,128)(2,1)S(1)} %get-tuple-element.15), channel_id=1, replica_groups=mesh['dp'=12,'x'=4,'y'=8,'core'=2] {'dp'}, dimensions={0} | all-to-all | bytes 49152 | tf_op jit(solution)/shard_map/all_to_all | solution.py:210
  78.7 3.3 %shard_map.71 = (bf16[12,128,128]{2,1,0:T(8,128)(2,1)S(1)}, bf16[1440,128]{1,0:T(8,128)(2,1)S(1)}) custom-call(bf16[12,136,128]{2,1,0:T(8,128)(2,1)S(1)} %all_to_all.31.rx_ref.rx2_ref, bf16[12,8,128]{2,1,0:T(8,128)(2,1)S(1)} %all_to_all.32.rx_ref, f32[1440,128]{1,0:T(8,128)S(1)} %get-tuple-element.16.v_ref, bf16[1536,128]{1,0:T(8,128)(2,1)S(1)} %get-tuple-element.17.eb_ref, ...), custom_call_target="tpu_custom_call" | custom-call | flops 1000000000 | bytes 4000000 | tf_op jit(solution)/shard_map/pallas_call | solution.py:211
  82.0 20.9 %all_to_all.33.rx_ref = bf16[12,128,128]{2,1,0:T(8,128)(2,1)S(1)} all-to-all(bf16[12,128,128]{2,1,0:T(8,128)(2,1)S(1)} %get-tuple-element.21), channel_id=1, replica_groups=mesh['dp'=12,'x'=4,'y'=8,'core'=2] {'dp'}, dimensions={0} | all-to-all | bytes 786432 | tf_op jit(solution)/shard_map/all_to_all | solution.py:217
  102.9 1.1 shard_map.72
  104.0 17.6 %all_to_all.34.terms_ref = bf16[64,16,128]{2,1,0:T(8,128)(2,1)S(1)} all-to-all(bf16[64,16,128]{2,1,0:T(8,128)(2,1)S(1)} %bitcast.5), channel_id=1, replica_groups=mesh['dp'=12,'x'=4,'y'=8,'core'=2] {'x','y','core'}, dimensions={0} | all-to-all | bytes 524288 | tf_op jit(solution)/shard_map/all_to_all | solution.py:221
  121.6 0.1 shard_map.73
  121.7 14.0 %all_to_all.35.shares_ref = bf16[12,16,128]{2,1,0:T(8,128)(2,1)S(1)} all-to-all(bf16[12,16,128]{2,1,0:T(8,128)(2,1)S(1)} %shard_map.73), channel_id=1, replica_groups=mesh['dp'=12,'x'=4,'y'=8,'core'=2] {'dp'}, dimensions={0} | all-to-all | bytes 98304 | tf_op jit(solution)/shard_map/all_to_all | solution.py:223
  135.7 0.6 shard_map.74
  (1 shorter events, 0.0 us)
Async XLA Ops:
  0.6 25.4 %copy-start.1 = (bf16[128,1024]{1,0:T(8,128)(2,1)S(1)}, bf16[128,1024]{1,0:T(8,128)(2,1)}, u32[]{:S(2)}) copy-start(bf16[128,1024]{1,0:T(8,128)(2,1)} %hq_ref.3) | copy-start | bytes 786436
  0.6 0.7 copy-start.2
  1.4 24.7 %copy-start.3 = (s32[4,32]{1,0:T(4,128)S(1)}, s32[4,32]{1,0:T(4,128)}, u32[]{:S(2)}) copy-start(s32[4,32]{1,0:T(4,128)} %neg_ref.1) | copy-start | bytes 1540
  1.4 24.7 %copy-start.4 = (s32[4,32]{1,0:T(4,128)S(1)}, s32[4,32]{1,0:T(4,128)}, u32[]{:S(2)}) copy-start(s32[4,32]{1,0:T(4,128)} %rank_ref.1) | copy-start | bytes 1540
  26.0 35.3 %copy-start = (bf16[1440,1024]{1,0:T(8,128)(2,1)S(1)}, bf16[1440,1024]{1,0:T(8,128)(2,1)}, u32[]{:S(2)}) copy-start(bf16[1440,1024]{1,0:T(8,128)(2,1)} %hp_ref.3) | copy-start | bytes 8847364

commit v7 on v6

--- a/solution.py
+++ b/solution.py
@@ -142,7 +142,7 @@
     dv_ref[...] = dv[...].astype(BF16)
 
 
-def grad_kernel(dp, hq_ref, hp_ref, w_ref, rx_ref, vt_ref, dvp_ref, gq_ref, gw_ref):
+def grad_kernel(dp, hq_ref, hp_ref, rx_ref, vt_ref, dvp_ref, dvq_ref, gw_ref):
     deq = rx_ref[0].astype(F32)
     for s in range(1, dp):
         deq = deq + rx_ref[s].astype(F32)
@@ -150,7 +150,7 @@
     r = lax.rsqrt(jnp.sum(vt * vt, axis=0, keepdims=True) + EPS)
     et = vt * r
     dvq = (r * (deq - et * jnp.sum(et * deq, axis=0, keepdims=True))).astype(BF16)
-    gq_ref[...] = contract(dvq, w_ref[...], ((0,), (1,))).astype(BF16)
+    dvq_ref[...] = dvq
     gwt = contract(dvp_ref[...], hp_ref[...], ((0,), (0,)))
     gwt = gwt + jnp.dot(dvq, hq_ref[...], preferred_element_type=F32)
     gw_ref[...] = gwt.T.astype(BF16)
@@ -165,7 +165,8 @@
         tx_ref[d] = sent
 
 
-def sum_kernel(shares_ref, out_ref):
+def last_kernel(shares_ref, dvq_ref, w_ref, gq_ref, out_ref):
+    gq_ref[...] = contract(dvq_ref[...], w_ref[...], ((0,), (1,))).astype(BF16)
     total = shares_ref[0].astype(F32)
     for d in range(1, shares_ref.shape[0]):
         total = total + shares_ref[d].astype(F32)
@@ -215,13 +216,13 @@
         gflop=1,
     )(rx2, rx3, v, eb, expo, sa, sb)
     rx4 = lax.all_to_all(tx4, "dp", 0, 0)
-    grad_queries, gw = call(
-        functools.partial(grad_kernel, dp), [((128, width), BF16), ((width, 128), BF16)], gflop=1
-    )(hq, hp, weight, rx4, vt, dvp)
+    dvq, gw = call(
+        functools.partial(grad_kernel, dp), [((128, 128), BF16), ((width, 128), BF16)], gflop=1
+    )(hq, hp, rx4, vt, dvp)
     terms = lax.all_to_all(gw.reshape(n_mp, rows, 128), MP, 0, 0)
     (tx5,) = call(share_kernel, [((dp, rows, 128), BF16)])(terms)
     shares = lax.all_to_all(tx5, "dp", 0, 0)
-    (grad_weight,) = call(sum_kernel, [((rows, 128), F32)])(shares)
+    grad_queries, grad_weight = call(last_kernel, [((128, width), BF16), ((rows, 128), F32)])(shares, dvq, weight)
     return grad_queries, grad_weight
 
 

time: 137 us -> 137 us (level)
  no operation moved by 1% of the time
where the time goes in v7:
time: 137 us; the launch traced here: 136 us
  blocking collectives  125 us (91%)
  Pallas kernels  9.99 us (7%)
    all_to_all x1, blocking collectives, on_device(): rx2 = lax.all_to_all(tx2, 'dp', 0, 0)  34.9 us
    all_to_all x1, blocking collectives, on_device(): weight = lax.all_to_all(sent, MP, 0, 0).reshape(width, 128)  24.6 us
    all_to_all x1, blocking collectives, on_device(): rx4 = lax.all_to_all(tx4, 'dp', 0, 0)  20.9 us
    all_to_all x1, blocking collectives, on_device(): terms = lax.all_to_all(gw.reshape(n_mp, rows, 128), MP, 0, 0)  17.6 us
    all_to_all x1, blocking collectives, on_device(): shares = lax.all_to_all(tx5, 'dp', 0, 0)  14 us
    all_to_all x1, blocking collectives, on_device(): rx3 = lax.all_to_all(tx3, 'dp', 0, 0)  12.9 us
    pallas_call x1, Pallas kernels, on_device(): call(functools.partial(score_kernel, dp), [((dp, 8, 128), BF16), ((n_p, 1...  4.52 us
    pallas_call x1, Pallas kernels, on_device(): call(functools.partial(passage_kernel, dp), [((dp, 128, 128), BF16), ((n_...  3.28 us

profile of v7, /device:TPU:6, one launch (start us, length us, event | category | flops | bytes accessed | tf_op | source)
XLA Modules:
  0.0 136.4 jit_solution(17840719321412082744)
XLA Ops:
  0.6 0.0 copy-start.1
  0.6 0.0 copy-start.2
  0.7 0.7 copy-done.2
  1.4 0.0 copy-start.3
  1.4 0.0 copy-start.4
  1.4 24.6 %all_to_all.30 = bf16[64,16,128]{2,1,0:T(8,128)(2,1)S(1)} all-to-all(bf16[64,16,128]{2,1,0:T(8,128)(2,1)S(1)} %shard_map.68), channel_id=1, replica_groups=mesh['dp'=12,'x'=4,'y'=8,'core'=2] {'x','y','core'}, dimensions={0} | all-to-all | bytes 524288 | tf_op jit(solution)/shard_map/all_to_all | solution.py:192
  26.0 0.0 copy-done.1
  26.0 0.0 copy-done.3
  26.0 0.0 copy-done.4
  26.0 0.0 copy-start
  26.0 0.3 shard_map.69
  26.4 34.9 %all_to_all.31.rx_ref.rx2_ref = bf16[12,136,128]{2,1,0:T(8,128)(2,1)S(1)} all-to-all(bf16[12,136,128]{2,1,0:T(8,128)(2,1)S(1)} %get-tuple-element.14), channel_id=1, replica_groups=mesh['dp'=12,'x'=4,'y'=8,'core'=2] {'dp'}, dimensions={0} | all-to-all | bytes 835584 | tf_op jit(solution)/shard_map/all_to_all | solution.py:196
  61.3 0.0 copy-done
  61.3 4.5 %shard_map.70 = (bf16[12,8,128]{2,1,0:T(8,128)(2,1)S(1)}, f32[1440,128]{1,0:T(8,128)S(1)}, bf16[1536,128]{1,0:T(8,128)(2,1)S(1)}, bf16[1536,1536]{1,0:T(8,128)(2...) custom-call(bf16[1440,1024]{1,0:T(8,128)(2,1)S(1)} %copy-done, bf16[1024,128]{1,0:T(8,128)(2,1)S(1)} %bitcast.3, ...), custom_call_target="tpu_custom_call" | custom-call | flops 2000000000 | bytes 4000000 | tf_op jit(solution)/shard_map/pallas_call | solution.py:197
  65.8 12.9 %all_to_all.32.rx_ref = bf16[12,8,128]{2,1,0:T(8,128)(2,1)S(1)} all-to-all(bf16[12,8,128]{2,1,0:T(8,128)(2,1)S(1)} %get-tuple-element.15), channel_id=1, replica_groups=mesh['dp'=12,'x'=4,'y'=8,'core'=2] {'dp'}, dimensions={0} | all-to-all | bytes 49152 | tf_op jit(solution)/shard_map/all_to_all | solution.py:211
  78.7 3.3 %shard_map.71 = (bf16[12,128,128]{2,1,0:T(8,128)(2,1)S(1)}, bf16[1440,128]{1,0:T(8,128)(2,1)S(1)}) custom-call(bf16[12,136,128]{2,1,0:T(8,128)(2,1)S(1)} %all_to_all.31.rx_ref.rx2_ref, bf16[12,8,128]{2,1,0:T(8,128)(2,1)S(1)} %all_to_all.32.rx_ref, f32[1440,128]{1,0:T(8,128)S(1)} %get-tuple-element.16.v_ref, bf16[1536,128]{1,0:T(8,128)(2,1)S(1)} %get-tuple-element.17.eb_ref, ...), custom_call_target="tpu_custom_call" | custom-call | flops 1000000000 | bytes 4000000 | tf_op jit(solution)/shard_map/pallas_call | solution.py:212
  82.0 20.9 %all_to_all.33.rx_ref = bf16[12,128,128]{2,1,0:T(8,128)(2,1)S(1)} all-to-all(bf16[12,128,128]{2,1,0:T(8,128)(2,1)S(1)} %get-tuple-element.21), channel_id=1, replica_groups=mesh['dp'=12,'x'=4,'y'=8,'core'=2] {'dp'}, dimensions={0} | all-to-all | bytes 786432 | tf_op jit(solution)/shard_map/all_to_all | solution.py:218
  102.9 0.8 shard_map.72
  103.7 17.6 %all_to_all.34.terms_ref = bf16[64,16,128]{2,1,0:T(8,128)(2,1)S(1)} all-to-all(bf16[64,16,128]{2,1,0:T(8,128)(2,1)S(1)} %bitcast.5), channel_id=1, replica_groups=mesh['dp'=12,'x'=4,'y'=8,'core'=2] {'x','y','core'}, dimensions={0} | all-to-all | bytes 524288 | tf_op jit(solution)/shard_map/all_to_all | solution.py:222
  121.4 0.1 shard_map.73
  121.4 14.0 %all_to_all.35.shares_ref = bf16[12,16,128]{2,1,0:T(8,128)(2,1)S(1)} all-to-all(bf16[12,16,128]{2,1,0:T(8,128)(2,1)S(1)} %shard_map.73), channel_id=1, replica_groups=mesh['dp'=12,'x'=4,'y'=8,'core'=2] {'dp'}, dimensions={0} | all-to-all | bytes 98304 | tf_op jit(solution)/shard_map/all_to_all | solution.py:224
  135.5 1.0 shard_map.74
  (1 shorter events, 0.0 us)
Async XLA Ops:
  0.6 25.4 %copy-start.1 = (bf16[128,1024]{1,0:T(8,128)(2,1)S(1)}, bf16[128,1024]{1,0:T(8,128)(2,1)}, u32[]{:S(2)}) copy-start(bf16[128,1024]{1,0:T(8,128)(2,1)} %hq_ref.3) | copy-start | bytes 786436
  0.6 0.7 copy-start.2
  1.4 24.7 %copy-start.3 = (s32[4,32]{1,0:T(4,128)S(1)}, s32[4,32]{1,0:T(4,128)}, u32[]{:S(2)}) copy-start(s32[4,32]{1,0:T(4,128)} %neg_ref.1) | copy-start | bytes 1540
  1.4 24.7 %copy-start.4 = (s32[4,32]{1,0:T(4,128)S(1)}, s32[4,32]{1,0:T(4,128)}, u32[]{:S(2)}) copy-start(s32[4,32]{1,0:T(4,128)} %rank_ref.1) | copy-start | bytes 1540
  26.0 35.3 %copy-start = (bf16[1440,1024]{1,0:T(8,128)(2,1)S(1)}, bf16[1440,1024]{1,0:T(8,128)(2,1)}, u32[]{:S(2)}) copy-start(bf16[1440,1024]{1,0:T(8,128)(2,1)} %hp_ref.3) | copy-start | bytes 8847364
